TPU v7x, 32 devices: a whole 2x2x4 slice. The times are simulated.
32 devices in a mesh: gx: 8 (over z, y), gy: 4 (over x, core).
Axes of the slice: x: 2, y: 2, z: 4, core: 2. Of those that a mesh axis runs over, the one named last changes fastest.
Arguments:
- right_side: float32 [2, 32, 32, 384], P(None, 'gx', 'gy'), may hold values from -6 to 6
- velocity_table: float32 [16], replicated, may hold values from 2500 to 5000
- layer_index: int32 [32, 32, 384], P('gx', 'gy'), may hold values from 0 to 15
- absorb_level: int32 [32, 32, 384], P('gx', 'gy'), may hold values from 0 to 3
Outputs:
- solution_field: float32 [2, 32, 32, 384], P(None, 'gx', 'gy')
All inputs are finite; a program needn't handle non-finite values.
Results may differ from a plain program's by a relative error of at most 0.0001.
Values sent between devices are 32-bit elements; how exact they have to be, the bound alone decides.
A program may use at most 64 MiB of HBM per device.

v0:
```python
import math

import jax
import jax.numpy as jnp
from jax import lax
from jax.sharding import PartitionSpec as P

NU = 2
NC = 8


OMEGA = 0.6
BETA = 0.5
ABSORB = 0.25
KH_FACTOR = 2.0 * math.pi * 6.0 * 20.0


def extended_2(block, sides, width):
    for axis, dim in sides:
        count = lax.axis_size(axis)
        forward = [(i, i + 1) for i in range(count - 1)]
        backward = [(target, source) for source, target in forward]
        low = lax.ppermute(
            lax.slice_in_dim(block, block.shape[dim] - width, None, axis=dim), axis, forward
        )
        high = lax.ppermute(lax.slice_in_dim(block, 0, width, axis=dim), axis, backward)
        block = jnp.concatenate([low, block, high], axis=dim)
    return block


def complex_product(first, second):
    return jnp.stack(
        [first[0] * second[0] - first[1] * second[1], first[0] * second[1] + first[1] * second[0]]
    )


def neighbour_sum(padded):
    total = padded[:, 2:, 1:-1, 1:-1] + padded[:, :-2, 1:-1, 1:-1]
    total = total + padded[:, 1:-1, 2:, 1:-1] + padded[:, 1:-1, :-2, 1:-1]
    total = total + padded[:, 1:-1, 1:-1, 2:] + padded[:, 1:-1, 1:-1, :-2]
    return total


def pad_faces(field):
    extended = extended_2(field, (("gx", 1), ("gy", 2)), 1)
    return jnp.pad(extended, ((0, 0), (0, 0), (0, 0), (1, 1)))


def pad_rows(field):
    extended = extended_2(field, (("gy", 2),), 1)
    return jnp.pad(extended, ((0, 0), (1, 1), (0, 0), (1, 1)))


def apply_operator(field, padded, shift_term, grid_level):
    return (6.0 * field - neighbour_sum(padded)) * 0.25**grid_level - complex_product(
        shift_term, field
    )


def restrict(field):
    size_x, size_y, size_z = (field.shape[1], field.shape[2], field.shape[3])
    return field.reshape(2, size_x // 2, 2, size_y // 2, 2, size_z // 2, 2).mean(axis=(2, 4, 6))


def prolong(field):
    return jnp.repeat(jnp.repeat(jnp.repeat(field, 2, 1), 2, 2), 2, 3)


def inverse_of(shift_term, grid_level):
    diag_real = 6.0 * 0.25**grid_level - shift_term[0]
    diag_imag = -shift_term[1]
    denom = diag_real * diag_real + diag_imag * diag_imag
    return jnp.stack([diag_real / denom, -diag_imag / denom])


def smooth(update, source, shift_term, inverse_diag, grid_level, sweeps, padder):
    for sweep in range(sweeps):
        image = apply_operator(update, padder(update), shift_term, grid_level)
        update = update + OMEGA * complex_product(inverse_diag, source - image)
    return update


def coarse_solve(source, shift_term, inverse_diag):
    row_source, row_shift, row_inverse = (
        lax.all_gather(source, "gx", axis=1, tiled=True),
        lax.all_gather(shift_term, "gx", axis=1, tiled=True),
        lax.all_gather(inverse_diag, "gx", axis=1, tiled=True),
    )
    result = smooth(jnp.zeros_like(row_source), row_source, row_shift, row_inverse, 2, NC, pad_rows)
    width = source.shape[1]
    return lax.dynamic_slice_in_dim(result, lax.axis_index("gx") * width, width, 1)


def vcycle(source, shifts, inverses, grid_level):
    if grid_level == 2:
        return coarse_solve(source, shifts[2], inverses[2])
    update = smooth(
        jnp.zeros_like(source),
        source,
        shifts[grid_level],
        inverses[grid_level],
        grid_level,
        NU,
        pad_faces,
    )
    residual = source - apply_operator(update, pad_faces(update), shifts[grid_level], grid_level)
    correction = vcycle(restrict(residual), shifts, inverses, grid_level + 1)
    update = update + prolong(correction)
    return smooth(
        update, source, shifts[grid_level], inverses[grid_level], grid_level, NU, pad_faces
    )


def local(right_side, velocity_table, layer_index, absorb_level):
    velocity = jnp.zeros(layer_index.shape, jnp.float32)
    for layer_number in range(velocity_table.shape[0]):
        velocity = jnp.where(layer_index == layer_number, velocity_table[layer_number], velocity)
    kh_square = (KH_FACTOR / velocity) ** 2
    damping = BETA + ABSORB * absorb_level.astype(jnp.float32)
    shift_zero = jnp.stack([kh_square, -kh_square * damping])
    shift_one = restrict(shift_zero)
    shift_two = restrict(shift_one)
    shifts = (shift_zero, shift_one, shift_two)
    inverses = (inverse_of(shift_zero, 0), inverse_of(shift_one, 1), inverse_of(shift_two, 2))
    first = vcycle(right_side, shifts, inverses, 0)
    residual = right_side - apply_operator(first, pad_faces(first), shift_zero, 0)
    first = first + vcycle(residual, shifts, inverses, 0)
    return first


def solution(mesh):
    placed = (P(None, "gx", "gy", None), P(), P("gx", "gy", None), P("gx", "gy", None))
    return jax.shard_map(
        local, mesh=mesh, in_specs=placed, out_specs=P(None, "gx", "gy", None), check_vma=False
    )
```

profile of v0, /device:TPU:0, one launch (start us, length us, event | category | flops | bytes accessed | tf_op | source)
XLA Modules:
  0.0 547.3 jit_solution(452604577570443355)
XLA Ops:
  0.0 4.9 collective-permute-start.13
  6.8 4.5 collective-permute-start.1
  16.5 10.7 %add_multiply_fusion = (f32[4,8,384]{2,1,0:T(8,128)S(1)}, f32[4,8,384]{2,1,0:T(8,128)S(1)}) fusion(s32[4,8,384]{2,1,0:T(8,128)} %param.7, f32[]{:T(128)} %bitcast.15, s32[4,8,384]{2,1,0:T(8,128)} %param.6, f32[]{:T(128)} %bitcast.14, f32[]{:T(128)} %bitcast.13, f32[]{:T(128)} %bitcast.12, f32[]{:T(128)} %bitcast.11, f32[]{:T(128)} %bitcast.10, f32[]{:T(128)} %bitcast.9, ...), kind=kLoop, calls=%fused_computation.334 | loop fusion | flops 479232 | bytes 196672 | tf_op jit(solution)/shard_map/mul | solution.py:120
  31.2 4.9 stack.438
  39.2 29.3 %all-gather.1 = f32[2,16,96]{2,0,1:T(2,128)S(1)} all-gather(f32[2,2,96]{2,0,1:T(2,128)S(1)} %copy.691), channel_id=3, replica_groups=mesh['gx'=8,'gy'=4] {'gx'}, dimensions={1}, use_global_device_ids=true | all-gather | bytes 13824 | tf_op jit(solution)/shard_map/all_gather | solution.py:86
  91.5 4.8 collective-permute-start.9
  107.7 8.1 %reshape.99 = f32[2,2,2,4,2,192,2]{6,5,4,3,2,1,0:T(8,128)} reshape(f32[2,4,8,384]{3,2,1,0:T(8,128)S(1)} %fusion.52) | data formatting | bytes 196608 | tf_op jit(solution)/shard_map/reshape | solution.py:62
  124.8 19.0 %all_gather.14 = f32[2,8,2,96]{3,2,1,0:T(2,128)S(1)} all-gather(f32[2,1,2,96]{3,2,1,0:T(2,128)S(1)} %pad_maximum_fusion.239), channel_id=1, replica_groups=mesh['gx'=8,'gy'=4] {'gx'}, dimensions={1}, use_global_device_ids=true | all-gather | bytes 13824 | tf_op jit(solution)/shard_map/all_gather | solution.py:87
  146.4 7.4 %collective-permute-done.18 = f32[2,4,1,192]{3,2,1,0:T(1,128)S(1)} collective-permute-done((f32[2,4,1,192]{3,2,1,0:T(1,128)S(1)}, f32[2,4,1,192]{3,2,1,0:T(1,128)S(1)}, u32[]{:S(2)}, u32[]{:S(2)}) %collective-permute-start.18) | collective-permute-done | bytes 6176 | tf_op jit(solution)/shard_map/ppermute | solution.py:26
  168.6 26.0 %all-gather = f32[2,16,96]{2,0,1:T(2,128)S(1)} all-gather(f32[2,2,96]{2,0,1:T(2,128)S(1)} %copy.689), channel_id=2, replica_groups=mesh['gx'=8,'gy'=4] {'gx'}, dimensions={1}, use_global_device_ids=true | all-gather | bytes 13824 | tf_op jit(solution)/shard_map/all_gather | solution.py:85
  198.0 4.3 collective-permute-done.27
  202.6 4.3 collective-permute-start.28
  249.8 4.5 collective-permute-done.40
  261.0 4.8 collective-permute-start.45
  319.8 4.6 collective-permute-start.59
  336.5 4.9 collective-permute-start.63
  352.9 5.1 collective-permute-start.67
  359.0 8.1 %reshape.103 = f32[2,2,2,4,2,192,2]{6,5,4,3,2,1,0:T(8,128)} reshape(f32[2,4,8,384]{3,2,1,0:T(8,128)S(1)} %fusion.22) | data formatting | bytes 196608 | tf_op jit(solution)/shard_map/reshape | solution.py:62
  384.9 5.0 collective-permute-done.70
  406.1 26.0 %all-gather.2 = f32[2,16,96]{2,0,1:T(2,128)S(1)} all-gather(f32[2,2,96]{2,0,1:T(2,128)S(1)} %copy.727), channel_id=4, replica_groups=mesh['gx'=8,'gy'=4] {'gx'}, dimensions={1}, use_global_device_ids=true | all-gather | bytes 13824 | tf_op jit(solution)/shard_map/all_gather | solution.py:85
  434.9 4.3 collective-permute-done.77
  439.5 4.3 collective-permute-start.78
  486.6 4.5 collective-permute-done.90
  497.9 4.8 collective-permute-start.95
  (523 shorter events, 335.1 us)
Async XLA Ops:
  0.0 79.5 %collective-permute-start.13 = (f32[2,1,4,192]{3,2,1,0:T(4,128)S(1)}, f32[2,1,4,192]{3,2,1,0:T(4,128)S(1)}, u32[]{:S(2)}, u32[]{:S(2)}) collective-permute-start(f32[2,1,4,192]{3,2,1,0:T(4,128)S(1)} %broadcast.233), channel_id=1, source_target_pairs={{0,4},{4,8},{8,12},{12,16},{16,20},{20,24},{24,28},{1,5},{5,9},{9,... | collective-permute-start | bytes 18440 | tf_op jit(solution)/shard_map/ppermute | solution.py:23
  4.9 76.0 %collective-permute-start.12 = (f32[2,1,4,192]{3,2,1,0:T(4,128)S(1)}, f32[2,1,4,192]{3,2,1,0:T(4,128)S(1)}, u32[]{:S(2)}, u32[]{:S(2)}) collective-permute-start(f32[2,1,4,192]{3,2,1,0:T(4,128)S(1)} %broadcast.233), channel_id=1, source_target_pairs={{4,0},{8,4},{12,8},{16,12},{20,16},{24,20},{28,24},{5,1},{9,5},{13... | collective-permute-start | bytes 18440 | tf_op jit(solution)/shard_map/ppermute | solution.py:26
  6.8 61.8 %collective-permute-start.1 = (f32[2,1,8,384]{3,2,1,0:T(8,128)}, f32[2,1,8,384]{3,2,1,0:T(8,128)S(1)}, u32[]{:S(2)}, u32[]{:S(2)}) collective-permute-start(f32[2,1,8,384]{3,2,1,0:T(8,128)} %broadcast.228), channel_id=1, source_target_pairs={{0,4},{4,8},{8,12},{12,16},{16,20},{20,24},{24,28},{1,5},{5,9},{9,... | collective-permute-start | bytes 73736 | tf_op jit(solution)/shard_map/ppermute | solution.py:23
  11.3 57.2 %collective-permute-start = (f32[2,1,8,384]{3,2,1,0:T(8,128)}, f32[2,1,8,384]{3,2,1,0:T(8,128)S(1)}, u32[]{:S(2)}, u32[]{:S(2)}) collective-permute-start(f32[2,1,8,384]{3,2,1,0:T(8,128)} %broadcast.228), channel_id=1, source_target_pairs={{4,0},{8,4},{12,8},{16,12},{20,16},{24,20},{28,24},{5,1},{9,5},{13... | collective-permute-start | bytes 73736 | tf_op jit(solution)/shard_map/ppermute | solution.py:26
  13.2 143.4 %collective-permute-start.25 = (f32[2,8,1,96]{3,2,1,0:T(1,128)}, f32[2,8,1,96]{3,2,1,0:T(1,128)S(1)}, u32[]{:S(2)}, u32[]{:S(2)}) collective-permute-start(f32[2,8,1,96]{3,2,1,0:T(1,128)} %broadcast.240), channel_id=1, source_target_pairs={{1,0},{2,1},{3,2},{5,4},{6,5},{7,6},{9,8},{10,9},{11,10},{13,12},{... | collective-permute-start | bytes 18440 | tf_op jit(solution)/shard_map/ppermute | solution.py:26
  70.0 6.7 %collective-permute-start.3 = (f32[2,6,1,384]{3,0,2,1:T(2,128)S(1)}, f32[2,6,1,384]{3,0,2,1:T(2,128)S(1)}, u32[]{:S(2)}, u32[]{:S(2)}) collective-permute-start(f32[2,6,1,384]{3,0,2,1:T(2,128)S(1)} %copy.673), channel_id=1, source_target_pairs={{0,1},{1,2},{2,3},{4,5},{5,6},{6,7},{8,9},{9,10},{10,11},{12,13},{... | collective-permute-start | bytes 55304 | tf_op jit(solution)/shard_map/ppermute | solution.py:23
  73.0 83.6 %collective-permute-start.24 = (f32[2,8,1,96]{3,2,1,0:T(1,128)}, f32[2,8,1,96]{3,2,1,0:T(1,128)S(1)}, u32[]{:S(2)}, u32[]{:S(2)}) collective-permute-start(f32[2,8,1,96]{3,2,1,0:T(1,128)} %broadcast.240), channel_id=1, source_target_pairs={{0,1},{1,2},{2,3},{4,5},{5,6},{6,7},{8,9},{9,10},{10,11},{12,13},{... | collective-permute-start | bytes 18440 | tf_op jit(solution)/shard_map/ppermute | solution.py:23
  79.5 5.7 %collective-permute-start.4 = (f32[2,1,8,384]{3,2,1,0:T(8,128)S(1)}, f32[2,1,8,384]{3,2,1,0:T(8,128)S(1)}, u32[]{:S(2)}, u32[]{:S(2)}) collective-permute-start(f32[2,1,8,384]{3,2,1,0:T(8,128)S(1)} %get-tuple-element.90), channel_id=1, source_target_pairs={{4,0},{8,4},{12,8},{16,12},{20,16},{24,20},{28,24},{5,1},{9,5},{13... | collective-permute-start | bytes 73736 | tf_op jit(solution)/shard_map/ppermute | solution.py:26
  80.9 15.4 %collective-permute-start.15 = (f32[2,4,1,192]{3,2,1,0:T(1,128)S(1)}, f32[2,4,1,192]{3,2,1,0:T(1,128)S(1)}, u32[]{:S(2)}, u32[]{:S(2)}) collective-permute-start(f32[2,4,1,192]{3,2,1,0:T(1,128)S(1)} %get-tuple-element.199), channel_id=1, source_target_pairs={{0,1},{1,2},{2,3},{4,5},{5,6},{6,7},{8,9},{9,10},{10,11},{12,13},{... | collective-permute-start | bytes 18440 | tf_op jit(solution)/shard_map/ppermute | solution.py:23
  89.7 7.9 %collective-permute-start.14 = (f32[2,4,1,192]{3,2,1,0:T(1,128)S(1)}, f32[2,4,1,192]{3,2,1,0:T(1,128)S(1)}, u32[]{:S(2)}, u32[]{:S(2)}) collective-permute-start(f32[2,4,1,192]{3,2,1,0:T(1,128)S(1)} %get-tuple-element.200), channel_id=1, source_target_pairs={{1,0},{2,1},{3,2},{5,4},{6,5},{7,6},{9,8},{10,9},{11,10},{13,12},{... | collective-permute-start | bytes 18440 | tf_op jit(solution)/shard_map/ppermute | solution.py:26
  91.5 6.3 %collective-permute-start.9 = (f32[2,1,8,384]{3,2,1,0:T(8,128)S(1)}, f32[2,1,8,384]{3,2,1,0:T(8,128)S(1)}, u32[]{:S(2)}, u32[]{:S(2)}) collective-permute-start(f32[2,1,8,384]{3,2,1,0:T(8,128)S(1)} %get-tuple-element.87), channel_id=1, source_target_pairs={{0,4},{4,8},{8,12},{12,16},{16,20},{20,24},{24,28},{1,5},{5,9},{9,... | collective-permute-start | bytes 73736 | tf_op jit(solution)/shard_map/ppermute | solution.py:23
  119.3 24.4 %collective-permute-start.17 = (f32[2,1,4,192]{3,2,1,0:T(4,128)S(1)}, f32[2,1,4,192]{3,2,1,0:T(4,128)S(1)}, u32[]{:S(2)}, u32[]{:S(2)}) collective-permute-start(f32[2,1,4,192]{3,2,1,0:T(4,128)S(1)} %get-tuple-element.249), channel_id=1, source_target_pairs={{0,4},{4,8},{8,12},{12,16},{16,20},{20,24},{24,28},{1,5},{5,9},{9,... | collective-permute-start | bytes 18440 | tf_op jit(solution)/shard_map/ppermute | solution.py:23
  123.5 20.3 %collective-permute-start.16 = (f32[2,1,4,192]{3,2,1,0:T(4,128)S(1)}, f32[2,1,4,192]{3,2,1,0:T(4,128)S(1)}, u32[]{:S(2)}, u32[]{:S(2)}) collective-permute-start(f32[2,1,4,192]{3,2,1,0:T(4,128)S(1)} %get-tuple-element.250), channel_id=1, source_target_pairs={{4,0},{8,4},{12,8},{16,12},{20,16},{24,20},{28,24},{5,1},{9,5},{13... | collective-permute-start | bytes 18440 | tf_op jit(solution)/shard_map/ppermute | solution.py:26
  145.1 8.7 %collective-permute-start.18 = (f32[2,4,1,192]{3,2,1,0:T(1,128)S(1)}, f32[2,4,1,192]{3,2,1,0:T(1,128)S(1)}, u32[]{:S(2)}, u32[]{:S(2)}) collective-permute-start(f32[2,4,1,192]{3,2,1,0:T(1,128)S(1)} %get-tuple-element.198), channel_id=1, source_target_pairs={{1,0},{2,1},{3,2},{5,4},{6,5},{7,6},{9,8},{10,9},{11,10},{13,12},{... | collective-permute-start | bytes 18440 | tf_op jit(solution)/shard_map/ppermute | solution.py:26
  248.4 5.8 %collective-permute-start.40 = (f32[2,1,4,192]{3,2,1,0:T(4,128)S(1)}, f32[2,1,4,192]{3,2,1,0:T(4,128)S(1)}, u32[]{:S(2)}, u32[]{:S(2)}) collective-permute-start(f32[2,1,4,192]{3,2,1,0:T(4,128)S(1)} %get-tuple-element.226), channel_id=1, source_target_pairs={{4,0},{8,4},{12,8},{16,12},{20,16},{24,20},{28,24},{5,1},{9,5},{13... | collective-permute-start | bytes 18440 | tf_op jit(solution)/shard_map/ppermute | solution.py:26
  261.0 6.2 %collective-permute-start.45 = (f32[2,1,4,192]{3,2,1,0:T(4,128)S(1)}, f32[2,1,4,192]{3,2,1,0:T(4,128)S(1)}, u32[]{:S(2)}, u32[]{:S(2)}) collective-permute-start(f32[2,1,4,192]{3,2,1,0:T(4,128)S(1)} %get-tuple-element.223), channel_id=1, source_target_pairs={{0,4},{4,8},{8,12},{12,16},{16,20},{20,24},{24,28},{1,5},{5,9},{9,... | collective-permute-start | bytes 18440 | tf_op jit(solution)/shard_map/ppermute | solution.py:23
  282.8 5.7 %collective-permute-start.48 = (f32[2,1,8,384]{3,2,1,0:T(8,128)S(1)}, f32[2,1,8,384]{3,2,1,0:T(8,128)S(1)}, u32[]{:S(2)}, u32[]{:S(2)}) collective-permute-start(f32[2,1,8,384]{3,2,1,0:T(8,128)S(1)} %get-tuple-element.86), channel_id=1, source_target_pairs={{4,0},{8,4},{12,8},{16,12},{20,16},{24,20},{28,24},{5,1},{9,5},{13... | collective-permute-start | bytes 73736 | tf_op jit(solution)/shard_map/ppermute | solution.py:26
  298.4 5.7 %collective-permute-start.52 = (f32[2,1,8,384]{3,2,1,0:T(8,128)S(1)}, f32[2,1,8,384]{3,2,1,0:T(8,128)S(1)}, u32[]{:S(2)}, u32[]{:S(2)}) collective-permute-start(f32[2,1,8,384]{3,2,1,0:T(8,128)S(1)} %get-tuple-element.84), channel_id=1, source_target_pairs={{4,0},{8,4},{12,8},{16,12},{20,16},{24,20},{28,24},{5,1},{9,5},{13... | collective-permute-start | bytes 73736 | tf_op jit(solution)/shard_map/ppermute | solution.py:26
  318.5 5.9 %collective-permute-start.58 = (f32[2,6,1,384]{3,0,2,1:T(2,128)S(1)}, f32[2,6,1,384]{3,0,2,1:T(2,128)S(1)}, u32[]{:S(2)}, u32[]{:S(2)}) collective-permute-start(f32[2,6,1,384]{3,0,2,1:T(2,128)S(1)} %copy.709), channel_id=1, source_target_pairs={{1,0},{2,1},{3,2},{5,4},{6,5},{7,6},{9,8},{10,9},{11,10},{13,12},{... | collective-permute-start | bytes 55304 | tf_op jit(solution)/shard_map/ppermute | solution.py:26
  335.2 6.2 %collective-permute-start.62 = (f32[2,6,1,384]{3,0,2,1:T(2,128)S(1)}, f32[2,6,1,384]{3,0,2,1:T(2,128)S(1)}, u32[]{:S(2)}, u32[]{:S(2)}) collective-permute-start(f32[2,6,1,384]{3,0,2,1:T(2,128)S(1)} %copy.715), channel_id=1, source_target_pairs={{1,0},{2,1},{3,2},{5,4},{6,5},{7,6},{9,8},{10,9},{11,10},{13,12},{... | collective-permute-start | bytes 55304 | tf_op jit(solution)/shard_map/ppermute | solution.py:26
  351.6 6.4 %collective-permute-start.66 = (f32[2,6,1,384]{3,0,2,1:T(2,128)S(1)}, f32[2,6,1,384]{3,0,2,1:T(2,128)S(1)}, u32[]{:S(2)}, u32[]{:S(2)}) collective-permute-start(f32[2,6,1,384]{3,0,2,1:T(2,128)S(1)} %copy.721), channel_id=1, source_target_pairs={{1,0},{2,1},{3,2},{5,4},{6,5},{7,6},{9,8},{10,9},{11,10},{13,12},{... | collective-permute-start | bytes 55304 | tf_op jit(solution)/shard_map/ppermute | solution.py:26
  383.5 6.3 %collective-permute-start.70 = (f32[2,4,1,192]{3,2,1,0:T(1,128)S(1)}, f32[2,4,1,192]{3,2,1,0:T(1,128)S(1)}, u32[]{:S(2)}, u32[]{:S(2)}) collective-permute-start(f32[2,4,1,192]{3,2,1,0:T(1,128)S(1)} %get-tuple-element.144), channel_id=1, source_target_pairs={{1,0},{2,1},{3,2},{5,4},{6,5},{7,6},{9,8},{10,9},{11,10},{13,12},{... | collective-permute-start | bytes 18440 | tf_op jit(solution)/shard_map/ppermute | solution.py:26
  485.3 5.8 %collective-permute-start.90 = (f32[2,1,4,192]{3,2,1,0:T(4,128)S(1)}, f32[2,1,4,192]{3,2,1,0:T(4,128)S(1)}, u32[]{:S(2)}, u32[]{:S(2)}) collective-permute-start(f32[2,1,4,192]{3,2,1,0:T(4,128)S(1)} %get-tuple-element.204), channel_id=1, source_target_pairs={{4,0},{8,4},{12,8},{16,12},{20,16},{24,20},{28,24},{5,1},{9,5},{13... | collective-permute-start | bytes 18440 | tf_op jit(solution)/shard_map/ppermute | solution.py:26
  497.9 6.2 %collective-permute-start.95 = (f32[2,1,4,192]{3,2,1,0:T(4,128)S(1)}, f32[2,1,4,192]{3,2,1,0:T(4,128)S(1)}, u32[]{:S(2)}, u32[]{:S(2)}) collective-permute-start(f32[2,1,4,192]{3,2,1,0:T(4,128)S(1)} %get-tuple-element.201), channel_id=1, source_target_pairs={{0,4},{4,8},{8,12},{12,16},{16,20},{20,24},{24,28},{1,5},{5,9},{9,... | collective-permute-start | bytes 18440 | tf_op jit(solution)/shard_map/ppermute | solution.py:23
  (88 other events, 611.1 us)
where the time goes:
time: 554 us; the launch traced here: 547 us
  starting transfers between devices  245 us (44%)
  waiting for transfers between devices  131 us (24%)
  blocking collectives  100 us (18%)
  other arithmetic  35.2 us (6%)
  local copies, waits for them, and re-layouts  32.5 us (6%)
    ppermute x53, starting transfers between devices, extended_2(): lax.ppermute(lax.slice_in_dim(block, block.shape[dim] - width, None, axis...  177 us
    ppermute x53, waiting for transfers between devices, extended_2(): lax.ppermute(lax.slice_in_dim(block, 0, width, axis=dim), axis, backward)  123 us
    ppermute x53, starting transfers between devices, extended_2(): lax.ppermute(lax.slice_in_dim(block, 0, width, axis=dim), axis, backward)  68.7 us
    all_gather x2, blocking collectives, coarse_solve(): lax.all_gather(source, 'gx', axis=1, tiled=True)  52 us
    all_gather x1, blocking collectives, coarse_solve(): lax.all_gather(shift_term, 'gx', axis=1, tiled=True)  29.3 us
    all_gather x1, blocking collectives, coarse_solve(): lax.all_gather(inverse_diag, 'gx', axis=1, tiled=True)  19 us
    reshape x2, local copies, waits for them, and re-layouts, restrict(): field.reshape(2, size_x // 2, 2, size_y // 2, 2, size_z // 2, 2)  16.1 us
  transfers between devices with their start and end apart: 106, of which 54 were waited for; matrix products, arithmetic and copies ran while one was open for 7% of the time, Pallas kernels for 0%

commit v1 on v0

v1 whole, which is shorter than its diff:
```python
import functools
import math

import jax
import jax.numpy as jnp
from jax import lax
from jax.experimental import pallas as pl
from jax.experimental.pallas import tpu as pltpu
from jax.sharding import PartitionSpec as P

NC = 8
OMEGA = 0.6
BETA = 0.5
ABSORB = 0.25
KH_FACTOR = 2.0 * math.pi * 6.0 * 20.0
MESH = pl.DeviceIdType.MESH
HIGHEST = lax.Precision.HIGHEST

STEPS = [(1, 0), (-1, 0), (0, 1), (0, -1), (1, 1), (1, -1), (-1, 1), (-1, -1)]
EXCHANGES = [
    (4, 2, 2),
    (2, 2, 1),
    (2, 2, 1), (4, 2, 1), (2, 2, 1), (2, 1, 1),
    (4, 3, 1),
    (2, 2, 1), (4, 2, 1), (2, 2, 1), (2, 1, 1),
]


def product(a, b):
    return a[0] * b[0] - a[1] * b[1], a[0] * b[1] + a[1] * b[0]


def dot(a, b):
    return jnp.dot(a, b, precision=HIGHEST, preferred_element_type=jnp.float32)


def iota(shape, dim):
    return lax.broadcasted_iota(jnp.int32, shape, dim)


def kernel(ngx, ngy, depth, *refs):
    rhs, table, layer, absorb, out = refs[:5]
    buffers = refs[5 : 5 + 5 * len(EXCHANGES)]
    (shift0, diag0, w0, wf0, upd0, upd0b, first, w1, diag1, wf1, g1, upd1, upd1b, padded, tiles0, tiles1,
     send_sem, recv_sem, tile_send, tile_recv) = refs[5 + 5 * len(EXCHANGES) :]
    gathered = (tiles0, tiles1)
    count = ngx * ngy
    gx, gy = lax.axis_index("gx"), lax.axis_index("gy")
    me = gx * ngy + gy
    f32 = jnp.float32

    barrier = pltpu.get_barrier_semaphore()

    def greet(k, carry):
        other = lax.rem(me + k, count)
        pl.semaphore_signal(barrier, inc=1, device_id=(other // ngy, lax.rem(other, ngy)), device_id_type=MESH)
        return carry

    lax.fori_loop(1, count, greet, 0)

    def exists(dx, dy):
        checks = []
        if dx > 0:
            checks.append(gx < ngx - 1)
        if dx < 0:
            checks.append(gx > 0)
        if dy > 0:
            checks.append(gy < ngy - 1)
        if dy < 0:
            checks.append(gy > 0)
        return functools.reduce(jnp.logical_and, checks)

    def views(k):
        return buffers[5 * k : 5 * k + 5]

    for k, (size, wide, fields) in enumerate(EXCHANGES):
        ext, _, _, low, high = views(k)

        def clear(ref, start, n):
            ref[pl.ds(start, n)] = jnp.zeros((n,) + ref.shape[1:], f32)

        @pl.when(gx == 0)
        def _():
            for ref in (ext, low, high):
                clear(ref, 0, wide)

        @pl.when(gx == ngx - 1)
        def _():
            for ref in (ext, low, high):
                clear(ref, wide + size, wide)

        @pl.when(gy == 0)
        def _():
            clear(low, 0, size + 2 * wide)

        @pl.when(gy == ngy - 1)
        def _():
            clear(high, 0, size + 2 * wide)

    def copy_of(k, d):
        size, wide, fields = EXCHANGES[k]
        ext, up, down, low, high = views(k)
        dx, dy = STEPS[d]
        if dy == 0:
            src = ext.at[pl.ds(size if dx > 0 else wide, wide)]
            dst = ext.at[pl.ds(0 if dx > 0 else wide + size, wide)]
        else:
            source, target = (up, low) if dy > 0 else (down, high)
            if dx == 0:
                src, dst = source, target.at[pl.ds(wide, size)]
            elif dx > 0:
                src, dst = source.at[pl.ds(size - wide, wide)], target.at[pl.ds(0, wide)]
            else:
                src, dst = source.at[pl.ds(0, wide)], target.at[pl.ds(wide + size, wide)]
        return pltpu.make_async_remote_copy(
            src_ref=src, dst_ref=dst, send_sem=send_sem.at[k, d], recv_sem=recv_sem.at[k, d],
            device_id=(gx + dx, gy + dy), device_id_type=MESH,
        )

    row8 = iota((8, depth), 0)

    def put(k, plane, field, pair):
        size, wide, fields = EXCHANGES[k]
        ext, up, down, low, high = views(k)
        re, im = pair
        ext[wide + plane, 2 * field] = re
        ext[wide + plane, 2 * field + 1] = im
        up[plane, field] = jnp.where(row8 < 4, pltpu.roll(re, 4, 0), im)
        down[plane, field] = jnp.where(row8 < 4, re, pltpu.roll(im, 4, 0))

    def start(k):
        for d in range(8):
            @pl.when(exists(*STEPS[d]))
            def _(d=d):
                copy_of(k, d).start()

    def receive(k):
        for d in range(8):
            dx, dy = STEPS[d]

            @pl.when(exists(-dx, -dy))
            def _(d=d):
                copy_of(k, d).wait_recv()

    def get(k, plane, field):
        size, wide, fields = EXCHANGES[k]
        ext, up, down, low, high = views(k)
        above, below = high[plane, field], low[plane, field]
        re = jnp.where(row8 < 4, above, pltpu.roll(below, 4, 0))
        im = jnp.where(row8 < 4, pltpu.roll(above, 4, 0), below)
        return (
            jnp.concatenate([ext[plane, 2 * field], re], axis=0),
            jnp.concatenate([ext[plane, 2 * field + 1], im], axis=0),
        )

    lane16 = iota((16, depth), 1)

    def around(before, mid, after, s):
        total = before + after + pltpu.roll(mid, s, 0) + pltpu.roll(mid, 16 - s, 0)
        total = total + jnp.where(lane16 >= s, pltpu.roll(mid, s, 1), 0.0)
        return total + jnp.where(lane16 < depth - s, pltpu.roll(mid, depth - s, 1), 0.0)

    def load(ref, plane, rows=16):
        return ref[plane, 0, :rows], ref[plane, 1, :rows]

    def store(ref, plane, pair):
        ref[plane, 0], ref[plane, 1] = pair

    def neighbours(ref, plane, s):
        return tuple(around(ref[plane - 1, c], ref[plane, c], ref[plane + 1, c], s) for c in range(2))

    def weight(diag, inside):
        denom = diag[0] * diag[0] + diag[1] * diag[1]
        scale = jnp.where(inside, OMEGA / denom, 0.0)
        return diag[0] * scale, -diag[1] * scale

    def first_two(wf_ref, w_ref, target, planes, s, c):
        for p in planes:
            wf, ns, w = load(wf_ref, p), neighbours(wf_ref, p, s), load(w_ref, p)
            part = product(w, ns)
            store(target, p, tuple(1.4 * a + c * b for a, b in zip(wf, part)))

    def sweep(ref, wf_ref, w_ref, planes, shift, s, c):
        for p in planes:
            e, ns = load(ref, p), neighbours(ref, p, s)
            part = product(load(w_ref, p + shift), ns)
            wf = load(wf_ref, p + shift)
            yield p, tuple(0.4 * a + b + c * d for a, b, d in zip(e, wf, part))

    def residual(source, ref, diag, p, s, c):
        ns, part = neighbours(ref, p, s), product(diag, load(ref, p))
        return tuple(f + c * n - q for f, n, q in zip(source, ns, part))

    lane8 = iota((8, depth), 1)

    def pair_mean(value):
        value = value + jnp.where(row8 % 2 == 0, pltpu.roll(value, 7, 0), pltpu.roll(value, 1, 0))
        other = jnp.where(lane8 % 2 == 0, pltpu.roll(value, depth - 1, 1), pltpu.roll(value, 1, 1))
        return (value + other) * 0.125

    shifts1 = []
    shifts = []
    for p in range(4):
        index = layer[p]
        velocity = jnp.zeros((8, depth), f32)
        for number in range(table.shape[0]):
            velocity = jnp.where(index == number, table[number], velocity)
        ratio = KH_FACTOR / velocity
        kh2 = ratio * ratio
        shift = (kh2, -kh2 * (BETA + ABSORB * absorb[p].astype(f32)))
        shifts.append(shift)
        put(0, p, 0, (rhs[0, p], rhs[1, p]))
        put(0, p, 1, shift)
        if p % 2 == 1:
            mean = tuple(pair_mean(shifts[p - 1][c] + shift[c]) for c in range(2))
            shifts1.append(mean)
            put(1, p // 2, 0, mean)
    pl.semaphore_wait(barrier, count - 1)
    start(0)
    start(1)

    spread = 0.25 * (iota((depth, 128), 0) // 4 == iota((depth, 128), 1)).astype(f32)
    widen = (iota((128, depth), 1) // 4 == iota((128, depth), 0)).astype(f32)
    rows2 = 2 * ngy
    slot = iota((96, 3 * 2 * rows2), 0)
    entry = iota((96, 3 * 2 * rows2), 1)
    inner = slot % 16
    offset = jnp.where(inner < 12, inner // 4, -1)
    expand = ((entry // rows2 == slot // 16) & (entry % rows2 == 2 * gy + offset)).astype(f32)

    shift2_sum = tuple(shifts1[0][c] + shifts1[1][c] for c in range(2))
    zero_plane = jnp.zeros((rows2, 128), f32)
    for c in range(2):
        padded[0, c] = zero_plane
        padded[ngx + 1, c] = zero_plane
    row2 = iota((ngx, rows2, 128), 1)
    block8 = iota((8, 128), 0) // 2

    def unpack(buffer, comp):
        planes = []
        for x in range(ngx):
            groups = []
            for q in range(0, ngy, 4):
                value = buffer[x * ngy + q]
                for j in range(1, min(4, ngy - q)):
                    value = jnp.where(block8 == (comp + j) % 4, buffer[x * ngy + q + j], value)
                groups.append(pltpu.roll(value, 8 - 2 * comp, 0) if comp else value)
            planes.append(jnp.concatenate(groups, axis=0)[:rows2] if len(groups) > 1 else groups[0][:rows2])
        return jnp.stack(planes)

    coarse = {}

    def coarsest(cycle, sums):
        buffer = gathered[cycle]
        stacked = jnp.concatenate(list(sums) + (list(shift2_sum) if cycle == 0 else []), axis=0)
        rows = stacked.shape[0]
        at, to = iota((8, rows), 1), iota((8, rows), 0)
        left = 0.125 * ((at // 4) == (to + 8 - 2 * lax.rem(gy, 4)) % 8).astype(f32)
        buffer[me] = dot(dot(left, stacked), spread)

        def send(k, carry):
            other = lax.rem(me + k, count)
            pltpu.make_async_remote_copy(
                src_ref=buffer.at[me], dst_ref=buffer.at[me],
                send_sem=tile_send.at[cycle], recv_sem=tile_recv.at[cycle],
                device_id=(other // ngy, lax.rem(other, ngy)), device_id_type=MESH,
            ).start()
            return carry

        lax.fori_loop(1, count, send, 0)

    def coarsest_finish(cycle):
        buffer = gathered[cycle]
        every = buffer.at[pl.ds(0, count - 1)]
        pltpu.make_async_copy(every, every, tile_recv.at[cycle]).wait()
        source = unpack(buffer, 0), unpack(buffer, 1)
        if cycle == 0:
            shift = unpack(buffer, 2), unpack(buffer, 3)
            coarse["w"] = weight((0.375 - shift[0], -shift[1]), shift[0] > 0.0)
        w = coarse["w"]
        wf = product(w, source)
        none = jnp.zeros((1, rows2, 128), f32)

        def total(e):
            result = jnp.concatenate([none, e[:-1]], axis=0) + jnp.concatenate([e[1:], none], axis=0)
            result = result + jnp.where(row2 > 0, pltpu.roll(e, 1, 1), 0.0)
            result = result + jnp.where(row2 < rows2 - 1, pltpu.roll(e, rows2 - 1, 1), 0.0)
            return result + pltpu.roll(e, 1, 2) + pltpu.roll(e, 127, 2)

        def step(_, e):
            part = product(w, (total(e[0]), total(e[1])))
            return tuple(0.4 * a + b + 0.0625 * d for a, b, d in zip(e, wf, part))

        e = lax.fori_loop(0, NC - 1, step, wf)
        for c in range(2):
            for x in range(ngx):
                padded[x + 1, c] = e[c][x]
        own = jnp.concatenate([padded[gx + i, c] for i in range(3) for c in range(2)], axis=0)
        wide = dot(dot(expand, own), widen)
        return [tuple(wide[32 * i + 16 * c : 32 * i + 16 * c + 16] for c in range(2)) for i in range(3)]

    def cycle_part(cycle, base):
        source1, update0, update1, solution1 = base, base + 1, base + 2, base + 3
        first_two(wf0, w0, upd0, range(1, 7), 1, 1.0)
        held = []
        for p in range(4):
            r = residual(load(first, p + 2), upd0, load(diag0, p + 2), p + 2, 1, 1.0)
            held.append(tuple(v[:8] for v in r))
            if p % 2 == 1:
                put(source1, p // 2, 0, tuple(pair_mean(held[p - 1][c] + held[p][c]) for c in range(2)))
        start(source1)
        for p in range(4):
            put(update0, p, 0, load(upd0, p + 2, 8))
        start(update0)
        if cycle == 0:
            receive(1)
            for p in range(6):
                shift = get(1, p, 0)
                diag = (1.5 - shift[0], -shift[1])
                store(diag1, p, diag)
                store(w1, p, weight(diag, shift[0] > 0.0))
        receive(source1)
        for p in range(6):
            source = get(source1, p, 0)
            store(g1, p, source)
            store(wf1, p, product(load(w1, p), source))
        first_two(wf1, w1, upd1, range(1, 5), 2, 0.25)
        left, right = [
            residual(load(g1, p), upd1, load(diag1, p), p, 2, 0.25) for p in (2, 3)
        ]
        coarsest(cycle, tuple(left[c][:8] + right[c][:8] for c in range(2)))
        for p in range(2):
            put(update1, p, 0, load(upd1, p + 2, 8))
        start(update1)
        receive(update1)
        receive(update0)
        correction = coarsest_finish(cycle)
        for p in range(6):
            e = get(update1, p, 0)
            store(upd1, p, tuple(a + b for a, b in zip(e, correction[p // 2])))
        for p, e in sweep(upd1, wf1, w1, range(1, 5), 0, 2, 0.25):
            store(upd1b, p, e)
        for p, e in sweep(upd1b, wf1, w1, range(2, 4), 0, 2, 0.25):
            put(solution1, p - 2, 0, tuple(v[:8] for v in e))
        start(solution1)
        receive(solution1)
        for p in range(4):
            extra = get(solution1, p, 0)
            for fine in (2 * p, 2 * p + 1):
                e = get(update0, fine, 0)
                store(upd0, fine, tuple(a + b for a, b in zip(e, extra)))
        for p, e in sweep(upd0, wf0, w0, range(1, 7), 0, 1, 1.0):
            store(upd0b, p, e)
        return sweep(upd0b, wf0, w0, range(2, 6), 0, 1, 1.0)

    receive(0)
    for p in range(8):
        source, shift = get(0, p, 0), get(0, p, 1)
        diag = (6.0 - shift[0], -shift[1])
        store(first, p, source)
        store(diag0, p, diag)
        w = weight(diag, shift[0] > 0.0)
        store(w0, p, w)
        store(wf0, p, product(w, source))
    kept = []
    for p, e in cycle_part(0, 2):
        put(6, p - 2, 0, tuple(v[:8] for v in e))
    start(6)
    receive(6)
    for p in range(10):
        store(shift0, p, get(6, p, 0))
    for p in range(8):
        r = residual(load(first, p), shift0, load(diag0, p), p + 1, 1, 1.0) if False else None
        ns = neighbours(shift0, p + 1, 1)
        part = product(load(diag0, p), load(shift0, p + 1))
        r = tuple(f + n - q for f, n, q in zip(load(first, p), ns, part))
        store(first, p, r)
        store(wf0, p, product(load(w0, p), r))
    ext6 = views(6)[0]
    for p, e in cycle_part(1, 7):
        for c in range(2):
            out[c, p - 2] = ext6[3 + p - 2, c] + e[c][:8]

    for k in range(len(EXCHANGES)):
        for d in range(8):
            @pl.when(exists(*STEPS[d]))
            def _(k=k, d=d):
                copy_of(k, d).wait_send()
    for cycle in range(2):
        every = gathered[cycle].at[pl.ds(0, count - 1)]
        pltpu.make_async_copy(every, every, tile_send.at[cycle]).wait()


def local(ngx, ngy, right_side, velocity_table, layer_index, absorb_level):
    depth = right_side.shape[-1]
    scratch = []
    for size, wide, fields in EXCHANGES:
        scratch += [
            pltpu.VMEM((size + 2 * wide, 2 * fields, 8, depth), jnp.float32),
            pltpu.VMEM((size, fields, 8, depth), jnp.float32),
            pltpu.VMEM((size, fields, 8, depth), jnp.float32),
            pltpu.VMEM((size + 2 * wide, fields, 8, depth), jnp.float32),
            pltpu.VMEM((size + 2 * wide, fields, 8, depth), jnp.float32),
        ]
    scratch += [pltpu.VMEM((n, 2, 16, depth), jnp.float32) for n in (10, 8, 8, 8, 8, 8, 8, 6, 6, 6, 6, 6, 6)]
    scratch += [pltpu.VMEM((ngx + 2, 2, 2 * ngy, 128), jnp.float32)]
    scratch += [pltpu.VMEM((ngx * ngy, 8, 128), jnp.float32)] * 2
    scratch += [pltpu.SemaphoreType.DMA((len(EXCHANGES), 8))] * 2
    scratch += [pltpu.SemaphoreType.DMA((2,))] * 2
    vmem = pl.BlockSpec(memory_space=pltpu.VMEM)
    return pl.pallas_call(
        functools.partial(kernel, ngx, ngy, depth),
        out_shape=jax.ShapeDtypeStruct(right_side.shape, jnp.float32),
        in_specs=[vmem, pl.BlockSpec(memory_space=pltpu.SMEM), vmem, vmem],
        out_specs=vmem,
        scratch_shapes=scratch,
        compiler_params=pltpu.CompilerParams(
            collective_id=0, has_side_effects=True, vmem_limit_bytes=32 * 1024 * 1024
        ),
    )(right_side, velocity_table, layer_index, absorb_level)


def solution(mesh):
    placed = (P(None, "gx", "gy", None), P(), P("gx", "gy", None), P("gx", "gy", None))
    return jax.shard_map(
        functools.partial(local, mesh.shape["gx"], mesh.shape["gy"]),
        mesh=mesh, in_specs=placed, out_specs=P(None, "gx", "gy", None), check_vma=False,
    )
```

time: 554 us -> 72.9 us (0.13); the launches traced: 547 us -> 72.6 us
  starting transfers between devices: 245 us -> 0 us
  waiting for transfers between devices: 131 us -> 0 us
  blocking collectives: 100 us -> 0 us
  Pallas kernels: 0 us -> 68.8 us
  other arithmetic: 35.2 us -> 0 us
  local copies, waits for them, and re-layouts: 32.5 us -> 3.79 us
    ppermute x106 -> x0, starting transfers between devices: 245 us -> none  [the longest x53 177 us: extended_2(): lax.ppermute(lax.slice_in_dim(block, block.shape[dim] - width, None, axis...]
    ppermute x106 -> x0, waiting for transfers between devices: 131 us -> none  [the longest x53 123 us: extended_2(): lax.ppermute(lax.slice_in_dim(block, 0, width, axis=dim), axis, backward)]
    all_gather x4 -> x0, blocking collectives: 100 us -> none  [the longest x2 52 us: coarse_solve(): lax.all_gather(source, 'gx', axis=1, tiled=True)]
    pallas_call x0 -> x1, Pallas kernels: none -> 68.8 us  [local(): pl.pallas_call(functools.partial(kernel, ngx, ngy, depth), out_shape=jax....]
    reshape x8 -> x0, local copies, waits for them, and re-layouts: 17.6 us -> none  [the longest x2 16.1 us: restrict(): field.reshape(2, size_x // 2, 2, size_y // 2, 2, size_z // 2, 2)]
    mul x7 -> x0, other arithmetic: 10.8 us -> none  [the longest x1 10.7 us: local(): shift_zero = jnp.stack([kh_square, -kh_square * damping])]
    reduce_sum x9 -> x0, other arithmetic: 10.1 us -> none  [restrict(): field.reshape(2, size_x // 2, 2, size_y // 2, 2, size_z // 2, 2)]
    another operation x8 -> x0, local copies, waits for them, and re-layouts: 9.25 us -> none  [the longest x2 8.02 us: local(): shift_zero = jnp.stack([kh_square, -kh_square * damping])]
  transfers between devices with their start and end apart: 106 -> 0, of which waited for: 54 -> 0; matrix products, arithmetic and copies ran while one was open for 7% -> 0% of each run, Pallas kernels for 0% -> 0%
where the time goes in v1:
time: 72.9 us; the launch traced here: 72.6 us
  Pallas kernels  68.8 us (94%)
  local copies, waits for them, and re-layouts  3.79 us (5%)
    pallas_call x1, Pallas kernels, local(): pl.pallas_call(functools.partial(kernel, ngx, ngy, depth), out_shape=jax....  68.8 us
    unnamed x9, local copies, waits for them, and re-layouts  3.79 us

profile of v1, /device:TPU:0, one launch (start us, length us, event | category | flops | bytes accessed | tf_op | source)
XLA Modules:
  0.0 72.6 jit_solution(1447437450512125492)
XLA Ops:
  0.0 0.0 copy-start
  0.0 0.9 %copy-done = f32[2,4,8,384]{3,2,1,0:T(8,128)S(1)} copy-done((f32[2,4,8,384]{3,2,1,0:T(8,128)S(1)}, f32[2,4,8,384]{3,2,1,0:T(8,128)}, u32[]{:S(2)}) %copy-start) | copy-done | bytes 98328
  0.9 0.0 copy-start.1
  0.9 0.8 %copy-done.1 = s32[4,8,384]{2,1,0:T(8,128)S(1)} copy-done((s32[4,8,384]{2,1,0:T(8,128)S(1)}, s32[4,8,384]{2,1,0:T(8,128)}, u32[]{:S(2)}) %copy-start.1) | copy-done | bytes 49176
  1.7 0.0 copy-start.2
  1.7 0.8 %copy-done.2 = s32[4,8,384]{2,1,0:T(8,128)S(1)} copy-done((s32[4,8,384]{2,1,0:T(8,128)S(1)}, s32[4,8,384]{2,1,0:T(8,128)}, u32[]{:S(2)}) %copy-start.2) | copy-done | bytes 49176
  2.5 0.0 copy-start.3
  2.5 0.7 copy-done.3
  3.1 68.8 %shard_map.46 = f32[2,4,8,384]{3,2,1,0:T(8,128)S(1)} custom-call(f32[2,4,8,384]{3,2,1,0:T(8,128)S(1)} %copy-done, f32[16]{0:T(128)S(1)} %copy-done.3, s32[4,8,384]{2,1,0:T(8,128)S(1)} %copy-done.1, s32[4,8,384]{2,1,0:T(8,128)S(1)} %copy-done.2), custom_call_target="tpu_custom_call" | custom-call | tf_op jit(solution)/shard_map/pallas_call | solution.py:411
  72.0 0.6 copy.6
Async XLA Ops:
  0.0 0.9 %copy-start = (f32[2,4,8,384]{3,2,1,0:T(8,128)S(1)}, f32[2,4,8,384]{3,2,1,0:T(8,128)}, u32[]{:S(2)}) copy-start(f32[2,4,8,384]{3,2,1,0:T(8,128)} %refs_0_.1) | copy-start | bytes 294916
  0.9 0.8 %copy-start.1 = (s32[4,8,384]{2,1,0:T(8,128)S(1)}, s32[4,8,384]{2,1,0:T(8,128)}, u32[]{:S(2)}) copy-start(s32[4,8,384]{2,1,0:T(8,128)} %refs_2_.1) | copy-start | bytes 147460
  1.7 0.8 %copy-start.2 = (s32[4,8,384]{2,1,0:T(8,128)S(1)}, s32[4,8,384]{2,1,0:T(8,128)}, u32[]{:S(2)}) copy-start(s32[4,8,384]{2,1,0:T(8,128)} %refs_3_.1) | copy-start | bytes 147460
  2.5 0.7 copy-start.3

commit v2 on v0

v2 whole, which is shorter than its diff:
```python
import functools
import math

import jax
import jax.numpy as jnp
from jax import lax
from jax.experimental import pallas as pl
from jax.experimental.pallas import tpu as pltpu
from jax.sharding import PartitionSpec as P

NC = 8
OMEGA = 0.6
BETA = 0.5
ABSORB = 0.25
KH_FACTOR = 2.0 * math.pi * 6.0 * 20.0
MESH = pl.DeviceIdType.MESH
HIGHEST = lax.Precision.HIGHEST

CORNERS = [(1, 1), (1, -1), (-1, 1), (-1, -1)]


def product(a, b):
    return a[0] * b[0] - a[1] * b[1], a[0] * b[1] + a[1] * b[0]


def dot(a, b):
    return jnp.dot(a, b, precision=HIGHEST, preferred_element_type=jnp.float32)


def iota(shape, dim):
    return lax.broadcasted_iota(jnp.int32, shape, dim)


def scratch_of(ngx, ngy, layers, depth):
    f32 = jnp.float32

    def vmem(*shape):
        return pltpu.VMEM(shape, f32)

    def dense():
        return dict(own=vmem(8, depth), got=vmem(4, 8, depth), cs=vmem(4, 2, 1, depth), cr=vmem(4, 2, 1, depth))

    cycles = [
        dict(
            source=dense(), fine=dense(), solution=dense(),
            far=vmem(2, 2, 8, depth), farown=vmem(2, 2, 8, depth),
            up=vmem(2, 8, depth), down=vmem(2, 8, depth), low=vmem(2, 8, depth), high=vmem(2, 8, depth),
            cs=vmem(4, 2, 1, depth), cr=vmem(4, 2, 1, depth), tiles=vmem(ngx * ngy, 8, 128),
        )
        for _ in range(2)
    ]
    return dict(
        rhs=vmem(2, 4, 8, depth), layer=pltpu.VMEM((4, 8, depth), jnp.int32),
        absorb=pltpu.VMEM((4, 8, depth), jnp.int32), table=pltpu.SMEM((layers,), f32),
        ewf=vmem(8, 2, 8, depth), ew=vmem(8, 2, 8, depth),
        up=vmem(4, 8, depth), down=vmem(4, 8, depth), low=vmem(4, 8, depth), high=vmem(4, 8, depth),
        cs=vmem(4, 4, 1, depth), cr=vmem(4, 4, 1, depth),
        coef1=dict(own=vmem(8, depth), got=vmem(4, 8, depth)),
        first=vmem(10, 2, 8, depth),
        fup=vmem(4, 8, depth), fdown=vmem(4, 8, depth), flow=vmem(4, 8, depth), fhigh=vmem(4, 8, depth),
        fcs=vmem(4, 6, 1, depth), fcr=vmem(4, 6, 1, depth),
        cycles=cycles,
        diag0=vmem(4, 2, 8, depth), source0=vmem(4, 2, 8, depth),
        wf0=vmem(8, 2, 16, depth), w0=vmem(8, 2, 16, depth), upd0=vmem(8, 2, 16, depth), upd0b=vmem(8, 2, 16, depth),
        first16=vmem(10, 2, 16, depth),
        diag1=vmem(2, 2, 8, depth), source1=vmem(2, 2, 8, depth),
        wf1=vmem(6, 2, 16, depth), w1=vmem(6, 2, 16, depth), upd1=vmem(6, 2, 16, depth), upd1b=vmem(6, 2, 16, depth),
        padded=vmem(ngx + 2, 2, 2 * ngy, 128),
        send_sem=pltpu.SemaphoreType.DMA((88,)), recv_sem=pltpu.SemaphoreType.DMA((88,)),
        tile_send=pltpu.SemaphoreType.DMA((2,)), tile_recv=pltpu.SemaphoreType.DMA((2,)),
        load_sem=pltpu.SemaphoreType.DMA((4,)),
    )


def kernel(ngx, ngy, depth, tree, rhs_in, table_in, layer_in, absorb_in, out, *scratch):
    m = jax.tree.unflatten(tree, scratch)
    count = ngx * ngy
    gx, gy = lax.axis_index("gx"), lax.axis_index("gy")
    me = gx * ngy + gy
    f32 = jnp.float32

    loads = [
        pltpu.make_async_copy(a, m[b], m["load_sem"].at[i])
        for i, (a, b) in enumerate(((layer_in, "layer"), (absorb_in, "absorb"), (table_in, "table"), (rhs_in, "rhs")))
    ]
    for load_copy in loads:
        load_copy.start()

    barrier = pltpu.get_barrier_semaphore()

    def greet(k, carry):
        other = lax.rem(me + k, count)
        pl.semaphore_signal(barrier, inc=1, device_id=(other // ngy, lax.rem(other, ngy)), device_id_type=MESH)
        return carry

    lax.fori_loop(1, count, greet, 0)

    def exists(dx, dy):
        checks = []
        if dx:
            checks.append(gx < ngx - 1 if dx > 0 else gx > 0)
        if dy:
            checks.append(gy < ngy - 1 if dy > 0 else gy > 0)
        return functools.reduce(jnp.logical_and, checks)

    plan = []

    def add(name, step, src, dst):
        plan.append((name, step, src, dst, len(plan)))

    def cut(ref, first, size=1):
        return ref.at[pl.ds(first, size)]

    def add_packets(name, up, down, low, high):
        add(name, (0, 1), up, low)
        add(name, (0, -1), down, high)

    def add_corners(name, cs, cr):
        for i, step in enumerate(CORNERS):
            add(name, step, cs.at[i], cr.at[i])

    def add_dense(name, b):
        for i, step in enumerate([(1, 0), (-1, 0), (0, 1), (0, -1)]):
            add(name, step, b["own"], b["got"].at[i])
        if "cs" in b:
            add_corners(name, b["cs"], b["cr"])

    add("begin", (1, 0), cut(m["ewf"], 4, 2), cut(m["ewf"], 0, 2))
    add("begin", (-1, 0), cut(m["ewf"], 2, 2), cut(m["ewf"], 6, 2))
    add("begin", (1, 0), cut(m["ew"], 5), cut(m["ew"], 1))
    add("begin", (-1, 0), cut(m["ew"], 2), cut(m["ew"], 6))
    add_packets("begin", m["up"], m["down"], m["low"], m["high"])
    add_corners("begin", m["cs"], m["cr"])
    add_dense("coef1", m["coef1"])
    add("later", (1, 0), cut(m["ew"], 4), cut(m["ew"], 0))
    add("later", (-1, 0), cut(m["ew"], 3), cut(m["ew"], 7))
    for cycle in range(2):
        b = m["cycles"][cycle]
        add_dense(f"source{cycle}", b["source"])
        add(f"update{cycle}", (1, 0), cut(b["farown"], 0), cut(b["far"], 0))
        add(f"update{cycle}", (-1, 0), cut(b["farown"], 1), cut(b["far"], 1))
        add_packets(f"update{cycle}", b["up"], b["down"], b["low"], b["high"])
        add_corners(f"update{cycle}", b["cs"], b["cr"])
        add_dense(f"fine{cycle}", b["fine"])
        add_dense(f"solution{cycle}", b["solution"])
    add("first", (1, 0), cut(m["first"], 4, 3), cut(m["first"], 0, 3))
    add("first", (-1, 0), cut(m["first"], 3, 3), cut(m["first"], 7, 3))
    add_packets("first", m["fup"], m["fdown"], m["flow"], m["fhigh"])
    add_corners("first", m["fcs"], m["fcr"])
    steps = sorted({entry[1] for entry in plan})

    for step in steps:
        @pl.when(jnp.logical_not(exists(-step[0], -step[1])))
        def _(step=step):
            for _, other, _, dst, _ in plan:
                if other == step:
                    dst[...] = jnp.zeros(dst.shape, f32)

    def remote(entry):
        _, (dx, dy), src, dst, i = entry
        return pltpu.make_async_remote_copy(
            src_ref=src, dst_ref=dst, send_sem=m["send_sem"].at[i], recv_sem=m["recv_sem"].at[i],
            device_id=(gx + dx, gy + dy), device_id_type=MESH,
        )

    def each(names, sign, act):
        for step in steps:
            mine = [entry for entry in plan if entry[0] in names and entry[1] == step]
            if mine:
                @pl.when(exists(sign * step[0], sign * step[1]))
                def _(mine=mine):
                    for entry in mine:
                        act(remote(entry))

    def start(*names):
        each(names, 1, lambda copy: copy.start())

    def receive(*names):
        each(names, -1, lambda copy: copy.wait_recv())

    row8, lane8, lane16 = iota((8, depth), 0), iota((8, depth), 1), iota((16, depth), 1)
    even_row, even_lane = row8 % 2 == 0, lane8 % 2 == 0

    def roll(value, shift, dim):
        size = value.shape[dim]
        return pltpu.roll(value, shift % size, dim) if shift % size else value

    def pack2(values, top):
        result = None
        for c, v in enumerate(values):
            v = roll(v, 2 * c + 2 if top else 2 * c, 0)
            result = v if c == 0 else jnp.where(row8 >= 2 * c, v, result)
        return result

    def unpack2(low, high, c):
        return jnp.where(row8 < 4, roll(high, -2 * c, 0), roll(low, 6 - 2 * c, 0))

    def pack4(pair, top):
        re, im = pair
        return jnp.where(row8 < 4, roll(re, 4, 0), im) if top else jnp.where(row8 < 4, re, roll(im, 4, 0))

    def unpack4(low, high):
        return jnp.where(row8 < 4, high, roll(low, 4, 0)), jnp.where(row8 < 4, roll(high, 4, 0), low)

    def put_corners(cs, j, near_low, near_high, from_edge):
        for i, (dx, dy) in enumerate(CORNERS):
            pair = near_high if dx > 0 else near_low
            at = 7 - from_edge if dy > 0 else from_edge
            for c, v in enumerate(pair):
                cs[i, j + c] = v[at : at + 1]

    def got_corner(cr, side, j):
        i = CORNERS.index((-side, 1))
        return cr[i, j], cr[i + 1, j]

    def corner_tile(cr, side, j, thick=1):
        below, above = got_corner(cr, side, j)
        return jnp.where(row8 >= 8 - thick, below, jnp.where(row8 < thick, above, 0.0))

    def pack_dense(first, second):
        return jnp.where(
            even_lane, jnp.where(even_row, first[0], first[1]), jnp.where(even_row, second[0], second[1])
        )

    def unpack_dense(tile):
        re = jnp.where(even_row, tile, roll(tile, 1, 0))
        im = jnp.where(even_row, roll(tile, -1, 0), tile)
        first = tuple(jnp.where(even_lane, v, roll(v, 1, 1)) for v in (re, im))
        second = tuple(jnp.where(even_lane, roll(v, -1, 1), v) for v in (re, im))
        return first, second

    def send_dense(b, planes):
        b["own"][...] = pack_dense(*planes)
        if "cs" in b:
            put_corners(b["cs"], 0, planes[0], planes[1], 0)

    def get_dense(b, own):
        before, after, below, above = [unpack_dense(b["got"][i]) for i in range(4)]
        none = jnp.zeros((8, depth), f32)
        result = []
        for p, plane in enumerate([*before, *own, *after]):
            pair = []
            for c in range(2):
                if p in (2, 3):
                    halo = jnp.where(row8 < 4, above[p - 2][c], below[p - 2][c])
                elif p in (1, 4) and "cr" in b:
                    halo = corner_tile(b["cr"], -1 if p == 1 else 1, c, 2)
                else:
                    halo = none
                pair.append(jnp.concatenate([plane[c], halo], axis=0))
            result.append(tuple(pair))
        return result

    def around(before, mid, after, s):
        total = before + after + roll(mid, s, 0) + roll(mid, -s, 0)
        total = total + jnp.where(lane16 >= s, roll(mid, s, 1), 0.0)
        return total + jnp.where(lane16 < depth - s, roll(mid, -s, 1), 0.0)

    def load(ref, plane, rows=None):
        return tuple(ref[plane, c] if rows is None else ref[plane, c, :rows] for c in range(2))

    def store(ref, plane, pair):
        ref[plane, 0], ref[plane, 1] = pair

    def neighbours(ref, plane, s):
        return tuple(around(ref[plane - 1, c], ref[plane, c], ref[plane + 1, c], s) for c in range(2))

    def weight(diag):
        scale = OMEGA / (diag[0] * diag[0] + diag[1] * diag[1])
        return diag[0] * scale, -diag[1] * scale

    def first_two(wf_ref, w_ref, target, planes, s, c):
        for p in planes:
            part = product(load(w_ref, p), neighbours(wf_ref, p, s))
            store(target, p, tuple(1.4 * a + c * b for a, b in zip(load(wf_ref, p), part)))

    def sweep(ref, wf_ref, w_ref, planes, s, c):
        for p in planes:
            part = product(load(w_ref, p), neighbours(ref, p, s))
            yield p, tuple(0.4 * a + b + c * d for a, b, d in zip(load(ref, p), load(wf_ref, p), part))

    def residual(source, diag, ref, p, s, c):
        ns, part = neighbours(ref, p, s), product(diag, load(ref, p, 8))
        return tuple(f + c * n[:8] - q for f, n, q in zip(source, ns, part))

    def pair_mean(value):
        value = value + jnp.where(even_row, roll(value, -1, 0), roll(value, 1, 0))
        other = jnp.where(even_lane, roll(value, -1, 1), roll(value, 1, 1))
        return (value + other) * 0.125

    def own8(pair):
        return tuple(v[:8] for v in pair)

    for load_copy in loads:
        load_copy.wait()
    shifts, weights, scaled = [], [], []
    for p in range(4):
        index = m["layer"][p]
        velocity = jnp.zeros((8, depth), f32)
        for number in range(m["table"].shape[0]):
            velocity = jnp.where(index == number, m["table"][number], velocity)
        ratio = KH_FACTOR / velocity
        kh2 = ratio * ratio
        shift = (kh2, -kh2 * (BETA + ABSORB * m["absorb"][p].astype(f32)))
        diag = (6.0 - shift[0], -shift[1])
        source = (m["rhs"][0, p], m["rhs"][1, p])
        w = weight(diag)
        wf = product(w, source)
        store(m["diag0"], p, diag)
        store(m["source0"], p, source)
        store(m["ewf"], p + 2, wf)
        store(m["ew"], p + 2, w)
        m["up"][p] = pack2([*wf, *w], True)
        m["down"][p] = pack2([*wf, *w], False)
        shifts.append(shift)
        weights.append(w)
        scaled.append(wf)
    put_corners(m["cs"], 0, scaled[0], scaled[3], 0)
    put_corners(m["cs"], 2, weights[0], weights[3], 0)
    pl.semaphore_wait(barrier, count - 1)
    start("begin")
    shifts1 = [tuple(pair_mean(shifts[p][c] + shifts[p + 1][c]) for c in range(2)) for p in (0, 2)]
    diags1 = [(1.5 - s[0], -s[1]) for s in shifts1]
    weights1 = [weight(d) for d in diags1]
    send_dense(m["coef1"], weights1)
    start("coef1", "later")
    for p in range(2):
        store(m["diag1"], p, diags1[p])

    spread = 0.25 * (iota((depth, 128), 0) // 4 == iota((depth, 128), 1)).astype(f32)
    widen = (iota((128, depth), 1) // 4 == iota((128, depth), 0)).astype(f32)
    rows2 = 2 * ngy
    slot, entry = iota((96, 6 * rows2), 0), iota((96, 6 * rows2), 1)
    inner = slot % 16
    offset = jnp.where(inner < 12, inner // 4, -1)
    expand = ((entry // rows2 == slot // 16) & (entry % rows2 == 2 * gy + offset)).astype(f32)

    shift2_sum = tuple(shifts1[0][c] + shifts1[1][c] for c in range(2))
    zero_plane = jnp.zeros((rows2, 128), f32)
    for c in range(2):
        m["padded"][0, c] = zero_plane
        m["padded"][ngx + 1, c] = zero_plane
    row2 = iota((ngx, rows2, 128), 1)
    block8 = iota((8, 128), 0) // 2

    def unpack(buffer, comp):
        planes = []
        for x in range(ngx):
            groups = []
            for q in range(0, ngy, 4):
                value = buffer[x * ngy + q]
                for j in range(1, min(4, ngy - q)):
                    value = jnp.where(block8 == (comp + j) % 4, buffer[x * ngy + q + j], value)
                groups.append(roll(value, -2 * comp, 0))
            planes.append(jnp.concatenate(groups, axis=0)[:rows2] if len(groups) > 1 else groups[0][:rows2])
        return jnp.stack(planes)

    coarse = {}

    def coarsest(cycle, sums):
        buffer = m["cycles"][cycle]["tiles"]
        stacked = jnp.concatenate(list(sums) + (list(shift2_sum) if cycle == 0 else []), axis=0)
        rows = stacked.shape[0]
        at, to = iota((8, rows), 1), iota((8, rows), 0)
        left = 0.125 * ((at // 4) == (to + 8 - 2 * lax.rem(gy, 4)) % 8).astype(f32)
        buffer[me] = dot(dot(left, stacked), spread)

        def send(k, carry):
            other = lax.rem(me + k, count)
            pltpu.make_async_remote_copy(
                src_ref=buffer.at[me], dst_ref=buffer.at[me],
                send_sem=m["tile_send"].at[cycle], recv_sem=m["tile_recv"].at[cycle],
                device_id=(other // ngy, lax.rem(other, ngy)), device_id_type=MESH,
            ).start()
            return carry

        lax.fori_loop(1, count, send, 0)

    def coarsest_finish(cycle):
        buffer = m["cycles"][cycle]["tiles"]
        every = buffer.at[pl.ds(0, count - 1)]
        pltpu.make_async_copy(every, every, m["tile_recv"].at[cycle]).wait()
        source = unpack(buffer, 0), unpack(buffer, 1)
        if cycle == 0:
            shift = unpack(buffer, 2), unpack(buffer, 3)
            full = weight((0.375 - shift[0], -shift[1]))
            coarse["w"] = tuple(jnp.where(shift[0] > 0.0, v, 0.0) for v in full)
        w = coarse["w"]
        wf = product(w, source)
        none = jnp.zeros((1, rows2, 128), f32)

        def total(e):
            result = jnp.concatenate([none, e[:-1]], axis=0) + jnp.concatenate([e[1:], none], axis=0)
            result = result + jnp.where(row2 > 0, roll(e, 1, 1), 0.0)
            result = result + jnp.where(row2 < rows2 - 1, roll(e, -1, 1), 0.0)
            return result + roll(e, 1, 2) + roll(e, -1, 2)

        def step(_, e):
            part = product(w, (total(e[0]), total(e[1])))
            return tuple(0.4 * a + b + 0.0625 * d for a, b, d in zip(e, wf, part))

        e = lax.fori_loop(0, NC - 1, step, wf)
        for c in range(2):
            for x in range(ngx):
                m["padded"][x + 1, c] = e[c][x]
        own = jnp.concatenate([m["padded"][gx + i, c] for i in range(3) for c in range(2)], axis=0)
        wide = dot(dot(expand, own), widen)
        return [tuple(wide[32 * i + 16 * c : 32 * i + 16 * c + 16] for c in range(2)) for i in range(3)]

    def cycle_part(cycle):
        b = m["cycles"][cycle]
        wf0, w0, upd0, upd0b = m["wf0"], m["w0"], m["upd0"], m["upd0b"]
        wf1, w1, upd1, upd1b = m["wf1"], m["w1"], m["upd1"], m["upd1b"]
        first_two(wf0, w0, upd0, range(1, 7), 1, 1.0)
        held = [residual(load(m["source0"], p), load(m["diag0"], p), upd0, p + 2, 1, 1.0) for p in range(4)]
        sources = [tuple(pair_mean(held[p][c] + held[p + 1][c]) for c in range(2)) for p in (0, 2)]
        scaled1 = [product(weights1[p], sources[p]) for p in range(2)]
        send_dense(b["source"], scaled1)
        start(f"source{cycle}")
        updates = [load(upd0, p + 2, 8) for p in range(4)]
        store(b["farown"], 0, updates[2])
        store(b["farown"], 1, updates[1])
        for i in range(2):
            b["up"][i] = pack2([*updates[2 * i], *updates[2 * i + 1]], True)
            b["down"][i] = pack2([*updates[2 * i], *updates[2 * i + 1]], False)
        put_corners(b["cs"], 0, updates[0], updates[3], 0)
        start(f"update{cycle}")
        if cycle == 0:
            receive("coef1")
            for p, pair in enumerate(get_dense(m["coef1"], weights1)):
                store(w1, p, pair)
        receive(f"source{cycle}")
        for p, pair in enumerate(get_dense(b["source"], scaled1)):
            store(wf1, p, pair)
        first_two(wf1, w1, upd1, range(1, 5), 2, 0.25)
        left, right = [residual(sources[p], load(m["diag1"], p), upd1, p + 2, 2, 0.25) for p in range(2)]
        coarsest(cycle, tuple(left[c] + right[c] for c in range(2)))
        updates1 = [load(upd1, p + 2, 8) for p in range(2)]
        send_dense(b["fine"], updates1)
        start(f"fine{cycle}")
        receive(f"update{cycle}", f"fine{cycle}")
        around1 = get_dense(b["fine"], updates1)
        none = jnp.zeros((8, depth), f32)
        for c in range(2):
            upd0[0, c] = jnp.concatenate([b["far"][0, c], none], axis=0)
            upd0[7, c] = jnp.concatenate([b["far"][1, c], none], axis=0)
            upd0[1, c, 8:] = corner_tile(b["cr"], -1, c)
            upd0[6, c, 8:] = corner_tile(b["cr"], 1, c)
            for p in range(4):
                upd0[p + 2, c, 8:] = unpack2(b["low"][p // 2], b["high"][p // 2], 2 * (p % 2) + c)
        correction = coarsest_finish(cycle)
        for p, e in enumerate(around1):
            store(upd1, p, tuple(v + x for v, x in zip(e, correction[p // 2])))
        for p, e in sweep(upd1, wf1, w1, range(1, 5), 2, 0.25):
            store(upd1b, p, e)
        solved = [own8(e) for _, e in sweep(upd1b, wf1, w1, range(2, 4), 2, 0.25)]
        send_dense(b["solution"], solved)
        start(f"solution{cycle}")
        receive(f"solution{cycle}")
        around1 = get_dense(b["solution"], solved)
        for p in range(8):
            store(upd0, p, tuple(v + x for v, x in zip(load(upd0, p), around1[p // 2 + 1])))
        for p, e in sweep(upd0, wf0, w0, range(1, 7), 1, 1.0):
            store(upd0b, p, e)
        for p, e in sweep(upd0b, wf0, w0, range(2, 6), 1, 1.0):
            yield p - 2, own8(e)

    none = jnp.zeros((8, depth), f32)

    def halo0(p, j):
        if p in (1, 6):
            return corner_tile(m["cr"], -1 if p == 1 else 1, j)
        if p in (0, 7):
            return none
        return unpack2(m["low"][p - 2], m["high"][p - 2], j)

    receive("begin")
    for p in range(8):
        for c in range(2):
            m["wf0"][p, c] = jnp.concatenate([m["ewf"][p, c], halo0(p, c)], axis=0)
            if p in (0, 7):
                m["w0"][p, c, 8:] = none
            else:
                m["w0"][p, c] = jnp.concatenate([m["ew"][p, c], halo0(p, 2 + c)], axis=0)
    kept = []
    for p, e in cycle_part(0):
        store(m["first"], p + 3, e)
        m["fup"][p] = pack4(e, True)
        m["fdown"][p] = pack4(e, False)
        kept.append(e)
    put_corners(m["fcs"], 0, kept[0], kept[3], 0)
    put_corners(m["fcs"], 2, kept[0], kept[3], 1)
    put_corners(m["fcs"], 4, kept[1], kept[2], 0)
    start("first")
    receive("first", "later")
    for p in (0, 7):
        for c in range(2):
            m["w0"][p, c, :8] = m["ew"][p, c]
    for p in range(10):
        if 3 <= p < 7:
            halo = unpack4(m["flow"][p - 3], m["fhigh"][p - 3])
        elif p in (2, 7):
            side, halo = (-1 if p == 2 else 1), []
            for c in range(2):
                below, above = got_corner(m["fcr"], side, c)
                below2, above2 = got_corner(m["fcr"], side, 2 + c)
                tile = jnp.where(row8 == 7, below, jnp.where(row8 == 6, below2, 0.0))
                halo.append(jnp.where(row8 == 0, above, jnp.where(row8 == 1, above2, tile)))
        elif p in (1, 8):
            halo = [corner_tile(m["fcr"], -1 if p == 1 else 1, 4 + c) for c in range(2)]
        else:
            halo = [none, none]
        for c in range(2):
            m["first16"][p, c] = jnp.concatenate([m["first"][p, c], halo[c]], axis=0)
    for p in range(8):
        ns = neighbours(m["first16"], p + 1, 1)
        e = load(m["first16"], p + 1)
        if 2 <= p < 6:
            part = product(load(m["diag0"], p - 2), own8(e))
            source = load(m["source0"], p - 2)
            store(m["source0"], p - 2, tuple(f + n[:8] - q for f, n, q in zip(source, ns, part)))
        part = product(load(m["w0"], p), ns)
        store(m["wf0"], p, tuple(a + b - OMEGA * v for a, b, v in zip(load(m["wf0"], p), part, e)))
    for p, e in cycle_part(1):
        for c in range(2):
            out[c, p] = m["first"][p + 3, c] + e[c]

    for step in steps:
        @pl.when(exists(*step))
        def _(step=step):
            for entry in plan:
                if entry[1] == step:
                    remote(entry).wait_send()
    for cycle in range(2):
        every = m["cycles"][cycle]["tiles"].at[pl.ds(0, count - 1)]
        pltpu.make_async_copy(every, every, m["tile_send"].at[cycle]).wait()


def local(ngx, ngy, right_side, velocity_table, layer_index, absorb_level):
    depth = right_side.shape[-1]
    scratch = scratch_of(ngx, ngy, velocity_table.shape[0], depth)
    leaves, tree = jax.tree.flatten(scratch)
    anywhere = pl.BlockSpec(memory_space=pl.ANY)
    return pl.pallas_call(
        functools.partial(kernel, ngx, ngy, depth, tree),
        out_shape=jax.ShapeDtypeStruct(right_side.shape, jnp.float32),
        in_specs=[anywhere] * 4,
        out_specs=pl.BlockSpec(memory_space=pltpu.VMEM),
        scratch_shapes=leaves,
        compiler_params=pltpu.CompilerParams(
            collective_id=0, has_side_effects=True, vmem_limit_bytes=48 * 1024 * 1024
        ),
    )(right_side, velocity_table, layer_index, absorb_level)


def solution(mesh):
    placed = (P(None, "gx", "gy", None), P(), P("gx", "gy", None), P("gx", "gy", None))
    return jax.shard_map(
        functools.partial(local, mesh.shape["gx"], mesh.shape["gy"]),
        mesh=mesh, in_specs=placed, out_specs=P(None, "gx", "gy", None), check_vma=False,
    )
```

time: 554 us -> 55.2 us (0.10); the launches traced: 547 us -> 55 us
  starting transfers between devices: 245 us -> 0 us
  waiting for transfers between devices: 131 us -> 0 us
  blocking collectives: 100 us -> 0 us
  Pallas kernels: 0 us -> 51.2 us
  other arithmetic: 35.2 us -> 0 us
  local copies, waits for them, and re-layouts: 32.5 us -> 3.79 us
    ppermute x106 -> x0, starting transfers between devices: 245 us -> none  [the longest x53 177 us: extended_2(): lax.ppermute(lax.slice_in_dim(block, block.shape[dim] - width, None, axis...]
    ppermute x106 -> x0, waiting for transfers between devices: 131 us -> none  [the longest x53 123 us: extended_2(): lax.ppermute(lax.slice_in_dim(block, 0, width, axis=dim), axis, backward)]
    all_gather x4 -> x0, blocking collectives: 100 us -> none  [the longest x2 52 us: coarse_solve(): lax.all_gather(source, 'gx', axis=1, tiled=True)]
    pallas_call x0 -> x1, Pallas kernels: none -> 51.2 us  [local(): pl.pallas_call(functools.partial(kernel, ngx, ngy, depth, tree), out_shap...]
    reshape x8 -> x0, local copies, waits for them, and re-layouts: 17.6 us -> none  [the longest x2 16.1 us: restrict(): field.reshape(2, size_x // 2, 2, size_y // 2, 2, size_z // 2, 2)]
    mul x7 -> x0, other arithmetic: 10.8 us -> none  [the longest x1 10.7 us: local(): shift_zero = jnp.stack([kh_square, -kh_square * damping])]
    reduce_sum x9 -> x0, other arithmetic: 10.1 us -> none  [restrict(): field.reshape(2, size_x // 2, 2, size_y // 2, 2, size_z // 2, 2)]
    another operation x8 -> x0, local copies, waits for them, and re-layouts: 9.25 us -> none  [the longest x2 8.02 us: local(): shift_zero = jnp.stack([kh_square, -kh_square * damping])]
  transfers between devices with their start and end apart: 106 -> 0, of which waited for: 54 -> 0; matrix products, arithmetic and copies ran while one was open for 7% -> 0% of each run, Pallas kernels for 0% -> 0%
where the time goes in v2:
time: 55.2 us; the launch traced here: 55 us
  Pallas kernels  51.2 us (93%)
  local copies, waits for them, and re-layouts  3.79 us (7%)
    pallas_call x1, Pallas kernels, local(): pl.pallas_call(functools.partial(kernel, ngx, ngy, depth, tree), out_shap...  51.2 us
    unnamed x9, local copies, waits for them, and re-layouts  3.79 us

profile of v2, /device:TPU:0, one launch (start us, length us, event | category | flops | bytes accessed | tf_op | source)
XLA Modules:
  0.0 55.0 jit_solution(4138113348036274316)
XLA Ops:
  0.0 0.0 copy-start
  0.0 0.9 %copy-done = f32[2,4,8,384]{3,2,1,0:T(8,128)S(1)} copy-done((f32[2,4,8,384]{3,2,1,0:T(8,128)S(1)}, f32[2,4,8,384]{3,2,1,0:T(8,128)}, u32[]{:S(2)}) %copy-start) | copy-done | bytes 98328
  0.9 0.0 copy-start.1
  0.9 0.8 %copy-done.1 = s32[4,8,384]{2,1,0:T(8,128)S(1)} copy-done((s32[4,8,384]{2,1,0:T(8,128)S(1)}, s32[4,8,384]{2,1,0:T(8,128)}, u32[]{:S(2)}) %copy-start.1) | copy-done | bytes 49176
  1.7 0.0 copy-start.2
  1.7 0.8 %copy-done.2 = s32[4,8,384]{2,1,0:T(8,128)S(1)} copy-done((s32[4,8,384]{2,1,0:T(8,128)S(1)}, s32[4,8,384]{2,1,0:T(8,128)}, u32[]{:S(2)}) %copy-start.2) | copy-done | bytes 49176
  2.5 0.0 copy-start.3
  2.5 0.7 %copy-done.3 = f32[16]{0:T(128)S(1)} copy-done((f32[16]{0:T(128)S(1)}, f32[16]{0:T(128)}, u32[]{:S(2)}) %copy-start.3) | copy-done | bytes 88
  3.1 51.2 %shard_map.46 = f32[2,4,8,384]{3,2,1,0:T(8,128)S(1)} custom-call(f32[2,4,8,384]{3,2,1,0:T(8,128)S(1)} %copy-done, f32[16]{0:T(128)S(1)} %copy-done.3, s32[4,8,384]{2,1,0:T(8,128)S(1)} %copy-done.1, s32[4,8,384]{2,1,0:T(8,128)S(1)} %copy-done.2), custom_call_target="tpu_custom_call" | custom-call | tf_op jit(solution)/shard_map/pallas_call | solution.py:544
  54.3 0.6 %copy.6 = f32[2,4,8,384]{3,2,1,0:T(8,128)} copy(f32[2,4,8,384]{3,2,1,0:T(8,128)S(1)} %shard_map.46) | data formatting | bytes 196608
Async XLA Ops:
  0.0 0.9 %copy-start = (f32[2,4,8,384]{3,2,1,0:T(8,128)S(1)}, f32[2,4,8,384]{3,2,1,0:T(8,128)}, u32[]{:S(2)}) copy-start(f32[2,4,8,384]{3,2,1,0:T(8,128)} %rhs_in.1) | copy-start | bytes 294916
  0.9 0.8 %copy-start.1 = (s32[4,8,384]{2,1,0:T(8,128)S(1)}, s32[4,8,384]{2,1,0:T(8,128)}, u32[]{:S(2)}) copy-start(s32[4,8,384]{2,1,0:T(8,128)} %layer_in.1) | copy-start | bytes 147460
  1.7 0.8 %copy-start.2 = (s32[4,8,384]{2,1,0:T(8,128)S(1)}, s32[4,8,384]{2,1,0:T(8,128)}, u32[]{:S(2)}) copy-start(s32[4,8,384]{2,1,0:T(8,128)} %absorb_in.1) | copy-start | bytes 147460
  2.5 0.7 %copy-start.3 = (f32[16]{0:T(128)S(1)}, f32[16]{0:T(128)}, u32[]{:S(2)}) copy-start(f32[16]{0:T(128)} %table_in.1) | copy-start | bytes 196

commit v3 on v2

--- a/solution.py
+++ b/solution.py
@@ -14,7 +14,6 @@
 ABSORB = 0.25
 KH_FACTOR = 2.0 * math.pi * 6.0 * 20.0
 MESH = pl.DeviceIdType.MESH
-HIGHEST = lax.Precision.HIGHEST
 
 CORNERS = [(1, 1), (1, -1), (-1, 1), (-1, -1)]
 
@@ -23,8 +22,16 @@
     return a[0] * b[0] - a[1] * b[1], a[0] * b[1] + a[1] * b[0]
 
 
-def dot(a, b):
-    return jnp.dot(a, b, precision=HIGHEST, preferred_element_type=jnp.float32)
+def dot3(a, b):
+    rows = a.shape[0]
+    pieces, rest = [], a
+    for _ in range(3):
+        piece = rest.astype(jnp.bfloat16).astype(jnp.float32)
+        pieces.append(piece)
+        rest = rest - piece
+    stacked = jnp.concatenate(pieces, axis=0).astype(jnp.bfloat16)
+    result = jnp.dot(stacked, b, preferred_element_type=jnp.float32)
+    return result[:rows] + result[rows : 2 * rows] + result[2 * rows :]
 
 
 def iota(shape, dim):
@@ -65,7 +72,7 @@
         first16=vmem(10, 2, 16, depth),
         diag1=vmem(2, 2, 8, depth), source1=vmem(2, 2, 8, depth),
         wf1=vmem(6, 2, 16, depth), w1=vmem(6, 2, 16, depth), upd1=vmem(6, 2, 16, depth), upd1b=vmem(6, 2, 16, depth),
-        padded=vmem(ngx + 2, 2, 2 * ngy, 128),
+        padded=vmem(ngx + 2, 2, 2 * ngy + 16, 128),
         send_sem=pltpu.SemaphoreType.DMA((88,)), recv_sem=pltpu.SemaphoreType.DMA((88,)),
         tile_send=pltpu.SemaphoreType.DMA((2,)), tile_recv=pltpu.SemaphoreType.DMA((2,)),
         load_sem=pltpu.SemaphoreType.DMA((4,)),
@@ -88,12 +95,22 @@
 
     barrier = pltpu.get_barrier_semaphore()
 
-    def greet(k, carry):
-        other = lax.rem(me + k, count)
-        pl.semaphore_signal(barrier, inc=1, device_id=(other // ngy, lax.rem(other, ngy)), device_id_type=MESH)
-        return carry
-
-    lax.fori_loop(1, count, greet, 0)
+    def others(act):
+        if count > 64:
+            def one(k, carry):
+                other = lax.rem(me + k, count)
+                act(other // ngy, lax.rem(other, ngy))
+                return carry
+
+            lax.fori_loop(1, count, one, 0)
+            return
+        for i in reversed(range(ngx)):
+            for j in reversed(range(ngy)):
+                if i or j:
+                    x, y = gx + i, gy + j
+                    act(jnp.where(x >= ngx, x - ngx, x), jnp.where(y >= ngy, y - ngy, y))
+
+    others(lambda x, y: pl.semaphore_signal(barrier, inc=1, device_id=(x, y), device_id_type=MESH))
 
     def exists(dx, dy):
         checks = []
@@ -328,18 +345,11 @@
         store(m["diag1"], p, diags1[p])
 
     spread = 0.25 * (iota((depth, 128), 0) // 4 == iota((depth, 128), 1)).astype(f32)
-    widen = (iota((128, depth), 1) // 4 == iota((128, depth), 0)).astype(f32)
+    spread = spread.astype(jnp.bfloat16)
+    widen = (iota((128, depth), 1) // 4 == iota((128, depth), 0)).astype(f32).astype(jnp.bfloat16)
     rows2 = 2 * ngy
-    slot, entry = iota((96, 6 * rows2), 0), iota((96, 6 * rows2), 1)
-    inner = slot % 16
-    offset = jnp.where(inner < 12, inner // 4, -1)
-    expand = ((entry // rows2 == slot // 16) & (entry % rows2 == 2 * gy + offset)).astype(f32)
-
     shift2_sum = tuple(shifts1[0][c] + shifts1[1][c] for c in range(2))
-    zero_plane = jnp.zeros((rows2, 128), f32)
-    for c in range(2):
-        m["padded"][0, c] = zero_plane
-        m["padded"][ngx + 1, c] = zero_plane
+    m["padded"][...] = jnp.zeros(m["padded"].shape, f32)
     row2 = iota((ngx, rows2, 128), 1)
     block8 = iota((8, 128), 0) // 2
 
@@ -359,22 +369,20 @@
 
     def coarsest(cycle, sums):
         buffer = m["cycles"][cycle]["tiles"]
-        stacked = jnp.concatenate(list(sums) + (list(shift2_sum) if cycle == 0 else []), axis=0)
-        rows = stacked.shape[0]
-        at, to = iota((8, rows), 1), iota((8, rows), 0)
-        left = 0.125 * ((at // 4) == (to + 8 - 2 * lax.rem(gy, 4)) % 8).astype(f32)
-        buffer[me] = dot(dot(left, stacked), spread)
-
-        def send(k, carry):
-            other = lax.rem(me + k, count)
-            pltpu.make_async_remote_copy(
+        tile = jnp.zeros((8, depth), f32)
+        for c, v in enumerate(list(sums) + (list(shift2_sum) if cycle == 0 else [])):
+            v = v + jnp.where(row8 // 2 % 2 == 0, roll(v, -2, 0), roll(v, 2, 0))
+            tile = jnp.where(row8 // 2 == c, roll(v, 2 * c - 3, 0), tile)
+        tile = dot3(tile * 0.25, spread)
+        buffer[me] = pltpu.roll(tile, 2 * lax.rem(gy, 4), 0)
+
+        others(
+            lambda x, y: pltpu.make_async_remote_copy(
                 src_ref=buffer.at[me], dst_ref=buffer.at[me],
                 send_sem=m["tile_send"].at[cycle], recv_sem=m["tile_recv"].at[cycle],
-                device_id=(other // ngy, lax.rem(other, ngy)), device_id_type=MESH,
+                device_id=(x, y), device_id_type=MESH,
             ).start()
-            return carry
-
-        lax.fori_loop(1, count, send, 0)
+        )
 
     def coarsest_finish(cycle):
         buffer = m["cycles"][cycle]["tiles"]
@@ -402,10 +410,19 @@
         e = lax.fori_loop(0, NC - 1, step, wf)
         for c in range(2):
             for x in range(ngx):
-                m["padded"][x + 1, c] = e[c][x]
-        own = jnp.concatenate([m["padded"][gx + i, c] for i in range(3) for c in range(2)], axis=0)
-        wide = dot(dot(expand, own), widen)
-        return [tuple(wide[32 * i + 16 * c : 32 * i + 16 * c + 16] for c in range(2)) for i in range(3)]
+                m["padded"][x + 1, c, 8 : 8 + rows2] = e[c][x]
+        own = [m["padded"][gx + i, c, pl.ds(7 + 2 * gy, 8)] for i in range(3) for c in range(2)]
+        wide = dot3(jnp.concatenate(own, axis=0), widen)
+        result = []
+        for i in range(3):
+            pair = []
+            for c in range(2):
+                below, low, high, above = [wide[16 * i + 8 * c + k : 16 * i + 8 * c + k + 1] for k in range(4)]
+                pair.append(
+                    jnp.concatenate([jnp.where(row8 < 4, low, high), jnp.where(row8 < 4, above, below)], axis=0)
+                )
+            result.append(tuple(pair))
+        return result
 
     def cycle_part(cycle):
         b = m["cycles"][cycle]
@@ -540,7 +557,7 @@
     depth = right_side.shape[-1]
     scratch = scratch_of(ngx, ngy, velocity_table.shape[0], depth)
     leaves, tree = jax.tree.flatten(scratch)
-    anywhere = pl.BlockSpec(memory_space=pl.ANY)
+    anywhere = pl.BlockSpec(memory_space=pltpu.HBM)
     return pl.pallas_call(
         functools.partial(kernel, ngx, ngy, depth, tree),
         out_shape=jax.ShapeDtypeStruct(right_side.shape, jnp.float32),
@@ -548,7 +565,7 @@
         out_specs=pl.BlockSpec(memory_space=pltpu.VMEM),
         scratch_shapes=leaves,
         compiler_params=pltpu.CompilerParams(
-            collective_id=0, has_side_effects=True, vmem_limit_bytes=48 * 1024 * 1024
+            collective_id=0, has_side_effects=True, vmem_limit_bytes=64 * 1024 * 1024 - 65536
         ),
     )(right_side, velocity_table, layer_index, absorb_level)
 

time: 55.2 us -> 52 us (0.942)
  local copies, waits for them, and re-layouts: 3.79 us -> 1.54 us
  Pallas kernels: 51.2 us -> 50.3 us
    unnamed x9 -> x1, local copies, waits for them, and re-layouts: 3.79 us -> 1.54 us
    pallas_call x1, Pallas kernels: 51.2 us -> 50.3 us  [local(): pl.pallas_call(functools.partial(kernel, ngx, ngy, depth, tree), out_shap...]
where the time goes in v3:
time: 52 us; the launch traced here: 51.8 us
  Pallas kernels  50.3 us (97%)
  local copies, waits for them, and re-layouts  1.54 us (3%)
    pallas_call x1, Pallas kernels, local(): pl.pallas_call(functools.partial(kernel, ngx, ngy, depth, tree), out_shap...  50.3 us
    unnamed x1, local copies, waits for them, and re-layouts  1.54 us

profile of v3, /device:TPU:0, one launch (start us, length us, event | category | flops | bytes accessed | tf_op | source)
XLA Modules:
  0.0 51.8 jit_solution(4740135802570189887)
XLA Ops:
  0.0 50.3 %shard_map.46 = f32[2,4,8,384]{3,2,1,0:T(8,128)} custom-call(f32[2,4,8,384]{3,2,1,0:T(8,128)} %rhs_in.1, f32[16]{0:T(128)} %table_in.1, s32[4,8,384]{2,1,0:T(8,128)} %layer_in.1, s32[4,8,384]{2,1,0:T(8,128)} %absorb_in.1), custom_call_target="tpu_custom_call" | custom-call | tf_op jit(solution)/shard_map/pallas_call | solution.py:561
  50.3 1.5 %copy.6 = f32[2,4,8,384]{3,2,1,0:T(8,128)} copy(f32[2,4,8,384]{3,2,1,0:T(8,128)} %shard_map.46) | data formatting | bytes 196608

commit v4 on v3

--- a/solution.py
+++ b/solution.py
@@ -15,6 +15,8 @@
 KH_FACTOR = 2.0 * math.pi * 6.0 * 20.0
 MESH = pl.DeviceIdType.MESH
 
+AROUND = [(dx, dy) for dx in range(-2, 3) for dy in (-1, 0, 1) if dx or dy]
+FACES = [(1, 0), (-1, 0), (0, 1), (0, -1)]
 CORNERS = [(1, 1), (1, -1), (-1, 1), (-1, -1)]
 
 
@@ -49,7 +51,7 @@
 
     cycles = [
         dict(
-            source=dense(), fine=dense(), solution=dense(),
+            source=dense(), fine=dict(own=vmem(8, depth), got=vmem(len(AROUND), 8, depth)), csource=vmem(4, 8, depth),
             far=vmem(2, 2, 8, depth), farown=vmem(2, 2, 8, depth),
             up=vmem(2, 8, depth), down=vmem(2, 8, depth), low=vmem(2, 8, depth), high=vmem(2, 8, depth),
             cs=vmem(4, 2, 1, depth), cr=vmem(4, 2, 1, depth), tiles=vmem(ngx * ngy, 8, 128),
@@ -62,7 +64,7 @@
         ewf=vmem(8, 2, 8, depth), ew=vmem(8, 2, 8, depth),
         up=vmem(4, 8, depth), down=vmem(4, 8, depth), low=vmem(4, 8, depth), high=vmem(4, 8, depth),
         cs=vmem(4, 4, 1, depth), cr=vmem(4, 4, 1, depth),
-        coef1=dict(own=vmem(8, depth), got=vmem(4, 8, depth)),
+        coef1=dict(own=vmem(8, depth), got=vmem(4, 8, depth)), ccoef1=vmem(4, 8, depth),
         first=vmem(10, 2, 8, depth),
         fup=vmem(4, 8, depth), fdown=vmem(4, 8, depth), flow=vmem(4, 8, depth), fhigh=vmem(4, 8, depth),
         fcs=vmem(4, 6, 1, depth), fcr=vmem(4, 6, 1, depth),
@@ -71,9 +73,11 @@
         wf0=vmem(8, 2, 16, depth), w0=vmem(8, 2, 16, depth), upd0=vmem(8, 2, 16, depth), upd0b=vmem(8, 2, 16, depth),
         first16=vmem(10, 2, 16, depth),
         diag1=vmem(2, 2, 8, depth), source1=vmem(2, 2, 8, depth),
-        wf1=vmem(6, 2, 16, depth), w1=vmem(6, 2, 16, depth), upd1=vmem(6, 2, 16, depth), upd1b=vmem(6, 2, 16, depth),
-        padded=vmem(ngx + 2, 2, 2 * ngy + 16, 128),
-        send_sem=pltpu.SemaphoreType.DMA((88,)), recv_sem=pltpu.SemaphoreType.DMA((88,)),
+        wf1=vmem(6, 2, 16, depth), w1=vmem(6, 2, 16, depth), upd1=vmem(6, 2, 16, depth),
+        wide_wf1=vmem(6, 2, 24, depth), wide_w1=vmem(6, 2, 24, depth),
+        wide1=vmem(8, 2, 24, depth), wide1b=vmem(8, 2, 24, depth),
+        padded=vmem(ngx + 4, 2, 2 * ngy + 16, 128),
+        send_sem=pltpu.SemaphoreType.DMA((112,)), recv_sem=pltpu.SemaphoreType.DMA((112,)),
         tile_send=pltpu.SemaphoreType.DMA((2,)), tile_recv=pltpu.SemaphoreType.DMA((2,)),
         load_sem=pltpu.SemaphoreType.DMA((4,)),
     )
@@ -115,7 +119,7 @@
     def exists(dx, dy):
         checks = []
         if dx:
-            checks.append(gx < ngx - 1 if dx > 0 else gx > 0)
+            checks.append(gx < ngx - dx if dx > 0 else gx >= -dx)
         if dy:
             checks.append(gy < ngy - 1 if dy > 0 else gy > 0)
         return functools.reduce(jnp.logical_and, checks)
@@ -137,7 +141,7 @@
             add(name, step, cs.at[i], cr.at[i])
 
     def add_dense(name, b):
-        for i, step in enumerate([(1, 0), (-1, 0), (0, 1), (0, -1)]):
+        for i, step in enumerate(FACES):
             add(name, step, b["own"], b["got"].at[i])
         if "cs" in b:
             add_corners(name, b["cs"], b["cr"])
@@ -149,6 +153,8 @@
     add_packets("begin", m["up"], m["down"], m["low"], m["high"])
     add_corners("begin", m["cs"], m["cr"])
     add_dense("coef1", m["coef1"])
+    for i, step in enumerate(CORNERS):
+        add("later1", step, m["coef1"]["own"], m["ccoef1"].at[i])
     add("later", (1, 0), cut(m["ew"], 4), cut(m["ew"], 0))
     add("later", (-1, 0), cut(m["ew"], 3), cut(m["ew"], 7))
     for cycle in range(2):
@@ -158,8 +164,10 @@
         add(f"update{cycle}", (-1, 0), cut(b["farown"], 1), cut(b["far"], 1))
         add_packets(f"update{cycle}", b["up"], b["down"], b["low"], b["high"])
         add_corners(f"update{cycle}", b["cs"], b["cr"])
-        add_dense(f"fine{cycle}", b["fine"])
-        add_dense(f"solution{cycle}", b["solution"])
+        for i, step in enumerate(AROUND):
+            add(f"fine{cycle}", step, b["fine"]["own"], b["fine"]["got"].at[i])
+        for i, step in enumerate(CORNERS):
+            add(f"fine{cycle}", step, b["source"]["own"], b["csource"].at[i])
     add("first", (1, 0), cut(m["first"], 4, 3), cut(m["first"], 0, 3))
     add("first", (-1, 0), cut(m["first"], 3, 3), cut(m["first"], 7, 3))
     add_packets("first", m["fup"], m["fdown"], m["flow"], m["fhigh"])
@@ -195,7 +203,7 @@
     def receive(*names):
         each(names, -1, lambda copy: copy.wait_recv())
 
-    row8, lane8, lane16 = iota((8, depth), 0), iota((8, depth), 1), iota((16, depth), 1)
+    row8, lane8 = iota((8, depth), 0), iota((8, depth), 1)
     even_row, even_lane = row8 % 2 == 0, lane8 % 2 == 0
 
     def roll(value, shift, dim):
@@ -270,8 +278,9 @@
 
     def around(before, mid, after, s):
         total = before + after + roll(mid, s, 0) + roll(mid, -s, 0)
-        total = total + jnp.where(lane16 >= s, roll(mid, s, 1), 0.0)
-        return total + jnp.where(lane16 < depth - s, roll(mid, -s, 1), 0.0)
+        lane = iota(mid.shape, 1)
+        total = total + jnp.where(lane >= s, roll(mid, s, 1), 0.0)
+        return total + jnp.where(lane < depth - s, roll(mid, -s, 1), 0.0)
 
     def load(ref, plane, rows=None):
         return tuple(ref[plane, c] if rows is None else ref[plane, c, :rows] for c in range(2))
@@ -291,10 +300,19 @@
             part = product(load(w_ref, p), neighbours(wf_ref, p, s))
             store(target, p, tuple(1.4 * a + c * b for a, b in zip(load(wf_ref, p), part)))
 
-    def sweep(ref, wf_ref, w_ref, planes, s, c):
+    def sweep(ref, wf_ref, w_ref, planes, s, c, behind=0):
         for p in planes:
-            part = product(load(w_ref, p), neighbours(ref, p, s))
-            yield p, tuple(0.4 * a + b + c * d for a, b, d in zip(load(ref, p), load(wf_ref, p), part))
+            part = product(load(w_ref, p - behind), neighbours(ref, p, s))
+            wf = load(wf_ref, p - behind)
+            yield p, tuple(0.4 * a + b + c * d for a, b, d in zip(load(ref, p), wf, part))
+
+    def wide_planes(tile_of, reach):
+        result = []
+        for rx in range(-reach, reach + 1):
+            blocks = [tile_of(rx, ry) for ry in (0, 1, -1)]
+            for half in range(2):
+                result.append(tuple(jnp.concatenate([v[half][c] for v in blocks], axis=0) for c in range(2)))
+        return result
 
     def residual(source, diag, ref, p, s, c):
         ns, part = neighbours(ref, p, s), product(diag, load(ref, p, 8))
@@ -340,7 +358,7 @@
     diags1 = [(1.5 - s[0], -s[1]) for s in shifts1]
     weights1 = [weight(d) for d in diags1]
     send_dense(m["coef1"], weights1)
-    start("coef1", "later")
+    start("coef1", "later", "later1")
     for p in range(2):
         store(m["diag1"], p, diags1[p])
 
@@ -410,24 +428,23 @@
         e = lax.fori_loop(0, NC - 1, step, wf)
         for c in range(2):
             for x in range(ngx):
-                m["padded"][x + 1, c, 8 : 8 + rows2] = e[c][x]
-        own = [m["padded"][gx + i, c, pl.ds(7 + 2 * gy, 8)] for i in range(3) for c in range(2)]
+                m["padded"][x + 2, c, 8 : 8 + rows2] = e[c][x]
+        own = [m["padded"][gx + i, c, pl.ds(6 + 2 * gy, 8)] for i in range(5) for c in range(2)]
         wide = dot3(jnp.concatenate(own, axis=0), widen)
         result = []
-        for i in range(3):
+        for i in range(5):
             pair = []
             for c in range(2):
-                below, low, high, above = [wide[16 * i + 8 * c + k : 16 * i + 8 * c + k + 1] for k in range(4)]
-                pair.append(
-                    jnp.concatenate([jnp.where(row8 < 4, low, high), jnp.where(row8 < 4, above, below)], axis=0)
-                )
+                rows = [wide[16 * i + 8 * c + k : 16 * i + 8 * c + k + 1] for k in (2, 3, 4, 5, 0, 1)]
+                tiles = [jnp.where(row8 < 4, rows[k], rows[k + 1]) for k in (0, 2, 4)]
+                pair.append(jnp.concatenate(tiles, axis=0))
             result.append(tuple(pair))
         return result
 
     def cycle_part(cycle):
         b = m["cycles"][cycle]
         wf0, w0, upd0, upd0b = m["wf0"], m["w0"], m["upd0"], m["upd0b"]
-        wf1, w1, upd1, upd1b = m["wf1"], m["w1"], m["upd1"], m["upd1b"]
+        wf1, w1, upd1 = m["wf1"], m["w1"], m["upd1"]
         first_two(wf0, w0, upd0, range(1, 7), 1, 1.0)
         held = [residual(load(m["source0"], p), load(m["diag0"], p), upd0, p + 2, 1, 1.0) for p in range(4)]
         sources = [tuple(pair_mean(held[p][c] + held[p + 1][c]) for c in range(2)) for p in (0, 2)]
@@ -453,10 +470,32 @@
         left, right = [residual(sources[p], load(m["diag1"], p), upd1, p + 2, 2, 0.25) for p in range(2)]
         coarsest(cycle, tuple(left[c] + right[c] for c in range(2)))
         updates1 = [load(upd1, p + 2, 8) for p in range(2)]
-        send_dense(b["fine"], updates1)
+        b["fine"]["own"][...] = pack_dense(*updates1)
         start(f"fine{cycle}")
+
+        def beside(own, faces, corners):
+            def tile_of(rx, ry):
+                step = (-rx, -ry)
+                if step == (0, 0):
+                    return own
+                return unpack_dense(faces[FACES.index(step)] if step in FACES else corners[CORNERS.index(step)])
+
+            return tile_of
+
+        if cycle == 0:
+            receive("later1")
+            tile_of = beside(weights1, m["coef1"]["got"], m["ccoef1"])
+            for p, pair in enumerate(wide_planes(tile_of, 1)):
+                store(m["wide_w1"], p, pair)
         receive(f"update{cycle}", f"fine{cycle}")
-        around1 = get_dense(b["fine"], updates1)
+        for p, pair in enumerate(wide_planes(beside(scaled1, b["source"]["got"], b["csource"]), 1)):
+            store(m["wide_wf1"], p, pair)
+        around1 = wide_planes(
+            lambda rx, ry: unpack_dense(b["fine"]["got"][AROUND.index((-rx, -ry))]) if rx or ry else updates1, 2
+        )
+        wide1, wide1b = m["wide1"], m["wide1b"]
+        for p in range(8):
+            store(wide1, p, around1[p + 1])
         none = jnp.zeros((8, depth), f32)
         for c in range(2):
             upd0[0, c] = jnp.concatenate([b["far"][0, c], none], axis=0)
@@ -466,17 +505,14 @@
             for p in range(4):
                 upd0[p + 2, c, 8:] = unpack2(b["low"][p // 2], b["high"][p // 2], 2 * (p % 2) + c)
         correction = coarsest_finish(cycle)
-        for p, e in enumerate(around1):
-            store(upd1, p, tuple(v + x for v, x in zip(e, correction[p // 2])))
-        for p, e in sweep(upd1, wf1, w1, range(1, 5), 2, 0.25):
-            store(upd1b, p, e)
-        solved = [own8(e) for _, e in sweep(upd1b, wf1, w1, range(2, 4), 2, 0.25)]
-        send_dense(b["solution"], solved)
-        start(f"solution{cycle}")
-        receive(f"solution{cycle}")
-        around1 = get_dense(b["solution"], solved)
         for p in range(8):
-            store(upd0, p, tuple(v + x for v, x in zip(load(upd0, p), around1[p // 2 + 1])))
+            store(wide1, p, tuple(v + x for v, x in zip(load(wide1, p), correction[(p + 1) // 2])))
+        for p, e in sweep(wide1, m["wide_wf1"], m["wide_w1"], range(1, 7), 2, 0.25, 1):
+            store(wide1b, p, e)
+        for p, e in sweep(wide1b, m["wide_wf1"], m["wide_w1"], range(2, 6), 2, 0.25, 1):
+            solved = [jnp.concatenate([v[:8], jnp.where(row8 < 4, v[8:16], v[16:24])], axis=0) for v in e]
+            for fine in (2 * p - 4, 2 * p - 3):
+                store(upd0, fine, tuple(v + x for v, x in zip(load(upd0, fine), solved)))
         for p, e in sweep(upd0, wf0, w0, range(1, 7), 1, 1.0):
             store(upd0b, p, e)
         for p, e in sweep(upd0b, wf0, w0, range(2, 6), 1, 1.0):

time: 52 us -> 48.2 us (0.927)
  Pallas kernels: 50.3 us -> 46.5 us
    pallas_call x1, Pallas kernels: 50.3 us -> 46.5 us  [local(): pl.pallas_call(functools.partial(kernel, ngx, ngy, depth, tree), out_shap...]
where the time goes in v4:
time: 48.2 us; the launch traced here: 48 us
  Pallas kernels  46.5 us (96%)
  local copies, waits for them, and re-layouts  1.54 us (3%)
    pallas_call x1, Pallas kernels, local(): pl.pallas_call(functools.partial(kernel, ngx, ngy, depth, tree), out_shap...  46.5 us
    unnamed x1, local copies, waits for them, and re-layouts  1.54 us

profile of v4, /device:TPU:0, one launch (start us, length us, event | category | flops | bytes accessed | tf_op | source)
XLA Modules:
  0.0 48.0 jit_solution(16277104780447051266)
XLA Ops:
  0.0 46.5 %shard_map.46 = f32[2,4,8,384]{3,2,1,0:T(8,128)} custom-call(f32[2,4,8,384]{3,2,1,0:T(8,128)} %rhs_in.1, f32[16]{0:T(128)} %table_in.1, s32[4,8,384]{2,1,0:T(8,128)} %layer_in.1, s32[4,8,384]{2,1,0:T(8,128)} %absorb_in.1), custom_call_target="tpu_custom_call" | custom-call | tf_op jit(solution)/shard_map/pallas_call | solution.py:597
  46.5 1.5 %copy.6 = f32[2,4,8,384]{3,2,1,0:T(8,128)} copy(f32[2,4,8,384]{3,2,1,0:T(8,128)} %shard_map.46) | data formatting | bytes 196608

commit v5 on v4

--- a/solution.py
+++ b/solution.py
@@ -167,7 +167,7 @@
         for i, step in enumerate(AROUND):
             add(f"fine{cycle}", step, b["fine"]["own"], b["fine"]["got"].at[i])
         for i, step in enumerate(CORNERS):
-            add(f"fine{cycle}", step, b["source"]["own"], b["csource"].at[i])
+            add(f"update{cycle}", step, b["source"]["own"], b["csource"].at[i])
     add("first", (1, 0), cut(m["first"], 4, 3), cut(m["first"], 0, 3))
     add("first", (-1, 0), cut(m["first"], 3, 3), cut(m["first"], 7, 3))
     add_packets("first", m["fup"], m["fdown"], m["flow"], m["fhigh"])
@@ -202,6 +202,9 @@
 
     def receive(*names):
         each(names, -1, lambda copy: copy.wait_recv())
+
+    def wait_sends(which):
+        each({entry[0] for entry in plan if which(entry[0])}, 1, lambda copy: copy.wait_send())
 
     row8, lane8 = iota((8, depth), 0), iota((8, depth), 1)
     even_row, even_lane = row8 % 2 == 0, lane8 % 2 == 0
@@ -487,15 +490,7 @@
             tile_of = beside(weights1, m["coef1"]["got"], m["ccoef1"])
             for p, pair in enumerate(wide_planes(tile_of, 1)):
                 store(m["wide_w1"], p, pair)
-        receive(f"update{cycle}", f"fine{cycle}")
-        for p, pair in enumerate(wide_planes(beside(scaled1, b["source"]["got"], b["csource"]), 1)):
-            store(m["wide_wf1"], p, pair)
-        around1 = wide_planes(
-            lambda rx, ry: unpack_dense(b["fine"]["got"][AROUND.index((-rx, -ry))]) if rx or ry else updates1, 2
-        )
-        wide1, wide1b = m["wide1"], m["wide1b"]
-        for p in range(8):
-            store(wide1, p, around1[p + 1])
+        receive(f"update{cycle}")
         none = jnp.zeros((8, depth), f32)
         for c in range(2):
             upd0[0, c] = jnp.concatenate([b["far"][0, c], none], axis=0)
@@ -504,9 +499,17 @@
             upd0[6, c, 8:] = corner_tile(b["cr"], 1, c)
             for p in range(4):
                 upd0[p + 2, c, 8:] = unpack2(b["low"][p // 2], b["high"][p // 2], 2 * (p % 2) + c)
+        for p, pair in enumerate(wide_planes(beside(scaled1, b["source"]["got"], b["csource"]), 1)):
+            store(m["wide_wf1"], p, pair)
+        wait_sends(lambda name: cycle == 1 and not name.startswith("fine1"))
         correction = coarsest_finish(cycle)
+        receive(f"fine{cycle}")
+        around1 = wide_planes(
+            lambda rx, ry: unpack_dense(b["fine"]["got"][AROUND.index((-rx, -ry))]) if rx or ry else updates1, 2
+        )
+        wide1, wide1b = m["wide1"], m["wide1b"]
         for p in range(8):
-            store(wide1, p, tuple(v + x for v, x in zip(load(wide1, p), correction[(p + 1) // 2])))
+            store(wide1, p, tuple(v + x for v, x in zip(around1[p + 1], correction[(p + 1) // 2])))
         for p, e in sweep(wide1, m["wide_wf1"], m["wide_w1"], range(1, 7), 2, 0.25, 1):
             store(wide1b, p, e)
         for p, e in sweep(wide1b, m["wide_wf1"], m["wide_w1"], range(2, 6), 2, 0.25, 1):
@@ -578,12 +581,7 @@
         for c in range(2):
             out[c, p] = m["first"][p + 3, c] + e[c]
 
-    for step in steps:
-        @pl.when(exists(*step))
-        def _(step=step):
-            for entry in plan:
-                if entry[1] == step:
-                    remote(entry).wait_send()
+    wait_sends(lambda name: name.startswith("fine1"))
     for cycle in range(2):
         every = m["cycles"][cycle]["tiles"].at[pl.ds(0, count - 1)]
         pltpu.make_async_copy(every, every, m["tile_send"].at[cycle]).wait()

time: 48.2 us -> 47.9 us (level)
  no operation moved by 1% of the time
where the time goes in v5:
time: 47.9 us; the launch traced here: 47.7 us
  Pallas kernels  46.2 us (96%)
  local copies, waits for them, and re-layouts  1.54 us (3%)
    pallas_call x1, Pallas kernels, local(): pl.pallas_call(functools.partial(kernel, ngx, ngy, depth, tree), out_shap...  46.2 us
    unnamed x1, local copies, waits for them, and re-layouts  1.54 us

profile of v5, /device:TPU:0, one launch (start us, length us, event | category | flops | bytes accessed | tf_op | source)
XLA Modules:
  0.0 47.7 jit_solution(11620426757267882889)
XLA Ops:
  0.0 46.2 %shard_map.46 = f32[2,4,8,384]{3,2,1,0:T(8,128)} custom-call(f32[2,4,8,384]{3,2,1,0:T(8,128)} %rhs_in.1, f32[16]{0:T(128)} %table_in.1, s32[4,8,384]{2,1,0:T(8,128)} %layer_in.1, s32[4,8,384]{2,1,0:T(8,128)} %absorb_in.1), custom_call_target="tpu_custom_call" | custom-call | tf_op jit(solution)/shard_map/pallas_call | solution.py:595
  46.2 1.5 %copy.6 = f32[2,4,8,384]{3,2,1,0:T(8,128)} copy(f32[2,4,8,384]{3,2,1,0:T(8,128)} %shard_map.46) | data formatting | bytes 196608

commit v6 on v5

--- a/solution.py
+++ b/solution.py
@@ -298,16 +298,28 @@
         scale = OMEGA / (diag[0] * diag[0] + diag[1] * diag[1])
         return diag[0] * scale, -diag[1] * scale
 
-    def first_two(wf_ref, w_ref, target, planes, s, c):
-        for p in planes:
+    def in_pairs(low, high, body):
+        def two(i, carry):
+            body(low + 2 * i)
+            body(low + 2 * i + 1)
+            return carry
+
+        lax.fori_loop(0, (high - low) // 2, two, 0)
+
+    def first_two(wf_ref, w_ref, target, low, high, s, c):
+        def body(p):
             part = product(load(w_ref, p), neighbours(wf_ref, p, s))
             store(target, p, tuple(1.4 * a + c * b for a, b in zip(load(wf_ref, p), part)))
 
-    def sweep(ref, wf_ref, w_ref, planes, s, c, behind=0):
-        for p in planes:
+        in_pairs(low, high, body)
+
+    def sweep(ref, wf_ref, w_ref, low, high, s, c, done, behind=0):
+        def body(p):
             part = product(load(w_ref, p - behind), neighbours(ref, p, s))
             wf = load(wf_ref, p - behind)
-            yield p, tuple(0.4 * a + b + c * d for a, b, d in zip(load(ref, p), wf, part))
+            done(p, tuple(0.4 * a + b + c * d for a, b, d in zip(load(ref, p), wf, part)))
+
+        in_pairs(low, high, body)
 
     def wide_planes(tile_of, reach):
         result = []
@@ -444,11 +456,11 @@
             result.append(tuple(pair))
         return result
 
-    def cycle_part(cycle):
+    def cycle_part(cycle, finish):
         b = m["cycles"][cycle]
         wf0, w0, upd0, upd0b = m["wf0"], m["w0"], m["upd0"], m["upd0b"]
         wf1, w1, upd1 = m["wf1"], m["w1"], m["upd1"]
-        first_two(wf0, w0, upd0, range(1, 7), 1, 1.0)
+        first_two(wf0, w0, upd0, 1, 7, 1, 1.0)
         held = [residual(load(m["source0"], p), load(m["diag0"], p), upd0, p + 2, 1, 1.0) for p in range(4)]
         sources = [tuple(pair_mean(held[p][c] + held[p + 1][c]) for c in range(2)) for p in (0, 2)]
         scaled1 = [product(weights1[p], sources[p]) for p in range(2)]
@@ -469,7 +481,7 @@
         receive(f"source{cycle}")
         for p, pair in enumerate(get_dense(b["source"], scaled1)):
             store(wf1, p, pair)
-        first_two(wf1, w1, upd1, range(1, 5), 2, 0.25)
+        first_two(wf1, w1, upd1, 1, 5, 2, 0.25)
         left, right = [residual(sources[p], load(m["diag1"], p), upd1, p + 2, 2, 0.25) for p in range(2)]
         coarsest(cycle, tuple(left[c] + right[c] for c in range(2)))
         updates1 = [load(upd1, p + 2, 8) for p in range(2)]
@@ -510,16 +522,18 @@
         wide1, wide1b = m["wide1"], m["wide1b"]
         for p in range(8):
             store(wide1, p, tuple(v + x for v, x in zip(around1[p + 1], correction[(p + 1) // 2])))
-        for p, e in sweep(wide1, m["wide_wf1"], m["wide_w1"], range(1, 7), 2, 0.25, 1):
-            store(wide1b, p, e)
-        for p, e in sweep(wide1b, m["wide_wf1"], m["wide_w1"], range(2, 6), 2, 0.25, 1):
+        sweep(
+            wide1, m["wide_wf1"], m["wide_w1"], 1, 7, 2, 0.25, lambda p, e: store(wide1b, p, e), behind=1
+        )
+
+        def prolong(p, e):
             solved = [jnp.concatenate([v[:8], jnp.where(row8 < 4, v[8:16], v[16:24])], axis=0) for v in e]
             for fine in (2 * p - 4, 2 * p - 3):
                 store(upd0, fine, tuple(v + x for v, x in zip(load(upd0, fine), solved)))
-        for p, e in sweep(upd0, wf0, w0, range(1, 7), 1, 1.0):
-            store(upd0b, p, e)
-        for p, e in sweep(upd0b, wf0, w0, range(2, 6), 1, 1.0):
-            yield p - 2, own8(e)
+
+        sweep(wide1b, m["wide_wf1"], m["wide_w1"], 2, 6, 2, 0.25, prolong, behind=1)
+        sweep(upd0, wf0, w0, 1, 7, 1, 1.0, lambda p, e: store(upd0b, p, e))
+        sweep(upd0b, wf0, w0, 2, 6, 1, 1.0, lambda p, e: finish(p - 2, own8(e)))
 
     none = jnp.zeros((8, depth), f32)
 
@@ -538,12 +552,14 @@
                 m["w0"][p, c, 8:] = none
             else:
                 m["w0"][p, c] = jnp.concatenate([m["ew"][p, c], halo0(p, 2 + c)], axis=0)
-    kept = []
-    for p, e in cycle_part(0):
+
+    def keep(p, e):
         store(m["first"], p + 3, e)
         m["fup"][p] = pack4(e, True)
         m["fdown"][p] = pack4(e, False)
-        kept.append(e)
+
+    cycle_part(0, keep)
+    kept = [load(m["first"], p + 3) for p in range(4)]
     put_corners(m["fcs"], 0, kept[0], kept[3], 0)
     put_corners(m["fcs"], 2, kept[0], kept[3], 1)
     put_corners(m["fcs"], 4, kept[1], kept[2], 0)
@@ -568,18 +584,22 @@
             halo = [none, none]
         for c in range(2):
             m["first16"][p, c] = jnp.concatenate([m["first"][p, c], halo[c]], axis=0)
-    for p in range(8):
-        ns = neighbours(m["first16"], p + 1, 1)
+    def next_source(p):
+        part = product(load(m["w0"], p), neighbours(m["first16"], p + 1, 1))
         e = load(m["first16"], p + 1)
-        if 2 <= p < 6:
-            part = product(load(m["diag0"], p - 2), own8(e))
-            source = load(m["source0"], p - 2)
-            store(m["source0"], p - 2, tuple(f + n[:8] - q for f, n, q in zip(source, ns, part)))
-        part = product(load(m["w0"], p), ns)
         store(m["wf0"], p, tuple(a + b - OMEGA * v for a, b, v in zip(load(m["wf0"], p), part, e)))
-    for p, e in cycle_part(1):
+
+    def next_own(p):
+        store(m["source0"], p, residual(load(m["source0"], p), load(m["diag0"], p), m["first16"], p + 3, 1, 1.0))
+
+    in_pairs(0, 8, next_source)
+    in_pairs(0, 4, next_own)
+
+    def give(p, e):
         for c in range(2):
             out[c, p] = m["first"][p + 3, c] + e[c]
+
+    cycle_part(1, give)
 
     wait_sends(lambda name: name.startswith("fine1"))
     for cycle in range(2):

time: 47.9 us -> 50.9 us (1.063)
  Pallas kernels: 46.2 us -> 49.2 us
    pallas_call x1, Pallas kernels: 46.2 us -> 49.2 us  [local(): pl.pallas_call(functools.partial(kernel, ngx, ngy, depth, tree), out_shap...]
where the time goes in v6:
time: 50.9 us; the launch traced here: 50.7 us
  Pallas kernels  49.2 us (97%)
  local copies, waits for them, and re-layouts  1.54 us (3%)
    pallas_call x1, Pallas kernels, local(): pl.pallas_call(functools.partial(kernel, ngx, ngy, depth, tree), out_shap...  49.2 us
    unnamed x1, local copies, waits for them, and re-layouts  1.54 us

profile of v6, /device:TPU:0, one launch (start us, length us, event | category | flops | bytes accessed | tf_op | source)
XLA Modules:
  0.0 50.7 jit_solution(17549994377964137918)
XLA Ops:
  0.0 49.2 %shard_map.46 = f32[2,4,8,384]{3,2,1,0:T(8,128)} custom-call(f32[2,4,8,384]{3,2,1,0:T(8,128)} %rhs_in.1, f32[16]{0:T(128)} %table_in.1, s32[4,8,384]{2,1,0:T(8,128)} %layer_in.1, s32[4,8,384]{2,1,0:T(8,128)} %absorb_in.1), custom_call_target="tpu_custom_call" | custom-call | tf_op jit(solution)/shard_map/pallas_call | solution.py:615
  49.2 1.5 %copy.6 = f32[2,4,8,384]{3,2,1,0:T(8,128)} copy(f32[2,4,8,384]{3,2,1,0:T(8,128)} %shard_map.46) | data formatting | bytes 196608

commit v7 on v5

--- a/solution.py
+++ b/solution.py
@@ -279,8 +279,9 @@
             result.append(tuple(pair))
         return result
 
-    def around(before, mid, after, s):
-        total = before + after + roll(mid, s, 0) + roll(mid, -s, 0)
+    def around(before, mid, after, s, rows):
+        beside = roll(mid, s, 0) + roll(mid, -s, 0)
+        total, mid = before + after + beside[:rows], mid[:rows]
         lane = iota(mid.shape, 1)
         total = total + jnp.where(lane >= s, roll(mid, s, 1), 0.0)
         return total + jnp.where(lane < depth - s, roll(mid, -s, 1), 0.0)
@@ -289,10 +290,14 @@
         return tuple(ref[plane, c] if rows is None else ref[plane, c, :rows] for c in range(2))
 
     def store(ref, plane, pair):
-        ref[plane, 0], ref[plane, 1] = pair
-
-    def neighbours(ref, plane, s):
-        return tuple(around(ref[plane - 1, c], ref[plane, c], ref[plane + 1, c], s) for c in range(2))
+        for c, v in enumerate(pair):
+            ref[plane, c, : v.shape[0]] = v
+
+    def neighbours(ref, plane, s, rows=None):
+        rows = rows or ref.shape[2]
+        return tuple(
+            around(ref[plane - 1, c, :rows], ref[plane, c], ref[plane + 1, c, :rows], s, rows) for c in range(2)
+        )
 
     def weight(diag):
         scale = OMEGA / (diag[0] * diag[0] + diag[1] * diag[1])
@@ -300,14 +305,16 @@
 
     def first_two(wf_ref, w_ref, target, planes, s, c):
         for p in planes:
-            part = product(load(w_ref, p), neighbours(wf_ref, p, s))
-            store(target, p, tuple(1.4 * a + c * b for a, b in zip(load(wf_ref, p), part)))
-
-    def sweep(ref, wf_ref, w_ref, planes, s, c, behind=0):
+            rows = 8 if p in (planes[0], planes[-1]) else 16
+            part = product(load(w_ref, p, rows), neighbours(wf_ref, p, s, rows))
+            store(target, p, tuple(1.4 * a + c * b for a, b in zip(load(wf_ref, p, rows), part)))
+
+    def sweep(ref, wf_ref, w_ref, planes, s, c, behind=0, rows_of=lambda p: None):
         for p in planes:
-            part = product(load(w_ref, p - behind), neighbours(ref, p, s))
-            wf = load(wf_ref, p - behind)
-            yield p, tuple(0.4 * a + b + c * d for a, b, d in zip(load(ref, p), wf, part))
+            rows = rows_of(p) or ref.shape[2]
+            part = product(load(w_ref, p - behind, rows), neighbours(ref, p, s, rows))
+            wf = load(wf_ref, p - behind, rows)
+            yield p, tuple(0.4 * a + b + c * d for a, b, d in zip(load(ref, p, rows), wf, part))
 
     def wide_planes(tile_of, reach):
         result = []
@@ -318,8 +325,8 @@
         return result
 
     def residual(source, diag, ref, p, s, c):
-        ns, part = neighbours(ref, p, s), product(diag, load(ref, p, 8))
-        return tuple(f + c * n[:8] - q for f, n, q in zip(source, ns, part))
+        ns, part = neighbours(ref, p, s, 8), product(diag, load(ref, p, 8))
+        return tuple(f + c * n - q for f, n, q in zip(source, ns, part))
 
     def pair_mean(value):
         value = value + jnp.where(even_row, roll(value, -1, 0), roll(value, 1, 0))
@@ -516,9 +523,9 @@
             solved = [jnp.concatenate([v[:8], jnp.where(row8 < 4, v[8:16], v[16:24])], axis=0) for v in e]
             for fine in (2 * p - 4, 2 * p - 3):
                 store(upd0, fine, tuple(v + x for v, x in zip(load(upd0, fine), solved)))
-        for p, e in sweep(upd0, wf0, w0, range(1, 7), 1, 1.0):
+        for p, e in sweep(upd0, wf0, w0, range(1, 7), 1, 1.0, rows_of=lambda p: 8 if p in (1, 6) else 16):
             store(upd0b, p, e)
-        for p, e in sweep(upd0b, wf0, w0, range(2, 6), 1, 1.0):
+        for p, e in sweep(upd0b, wf0, w0, range(2, 6), 1, 1.0, rows_of=lambda p: 8):
             yield p - 2, own8(e)
 
     none = jnp.zeros((8, depth), f32)
@@ -569,14 +576,15 @@
         for c in range(2):
             m["first16"][p, c] = jnp.concatenate([m["first"][p, c], halo[c]], axis=0)
     for p in range(8):
-        ns = neighbours(m["first16"], p + 1, 1)
-        e = load(m["first16"], p + 1)
+        rows = 8 if p in (0, 7) else 16
+        ns = neighbours(m["first16"], p + 1, 1, rows)
+        e = load(m["first16"], p + 1, rows)
         if 2 <= p < 6:
             part = product(load(m["diag0"], p - 2), own8(e))
             source = load(m["source0"], p - 2)
             store(m["source0"], p - 2, tuple(f + n[:8] - q for f, n, q in zip(source, ns, part)))
-        part = product(load(m["w0"], p), ns)
-        store(m["wf0"], p, tuple(a + b - OMEGA * v for a, b, v in zip(load(m["wf0"], p), part, e)))
+        part = product(load(m["w0"], p, rows), ns)
+        store(m["wf0"], p, tuple(a + b - OMEGA * v for a, b, v in zip(load(m["wf0"], p, rows), part, e)))
     for p, e in cycle_part(1):
         for c in range(2):
             out[c, p] = m["first"][p + 3, c] + e[c]

time: 47.9 us -> 47.8 us (level)
  no operation moved by 1% of the time
where the time goes in v7:
time: 47.8 us; the launch traced here: 47.6 us
  Pallas kernels  46 us (96%)
  local copies, waits for them, and re-layouts  1.54 us (3%)
    pallas_call x1, Pallas kernels, local(): pl.pallas_call(functools.partial(kernel, ngx, ngy, depth, tree), out_shap...  46 us
    unnamed x1, local copies, waits for them, and re-layouts  1.54 us

profile of v7, /device:TPU:0, one launch (start us, length us, event | category | flops | bytes accessed | tf_op | source)
XLA Modules:
  0.0 47.6 jit_solution(1532945347148233038)
XLA Ops:
  0.0 46.0 %shard_map.46 = f32[2,4,8,384]{3,2,1,0:T(8,128)} custom-call(f32[2,4,8,384]{3,2,1,0:T(8,128)} %rhs_in.1, f32[16]{0:T(128)} %table_in.1, s32[4,8,384]{2,1,0:T(8,128)} %layer_in.1, s32[4,8,384]{2,1,0:T(8,128)} %absorb_in.1), custom_call_target="tpu_custom_call" | custom-call | tf_op jit(solution)/shard_map/pallas_call | solution.py:603
  46.0 1.5 %copy.6 = f32[2,4,8,384]{3,2,1,0:T(8,128)} copy(f32[2,4,8,384]{3,2,1,0:T(8,128)} %shard_map.46) | data formatting | bytes 196608

commit v8 on v7

--- a/solution.py
+++ b/solution.py
@@ -435,7 +435,9 @@
             part = product(w, (total(e[0]), total(e[1])))
             return tuple(0.4 * a + b + 0.0625 * d for a, b, d in zip(e, wf, part))
 
-        e = lax.fori_loop(0, NC - 1, step, wf)
+        e = wf
+        for k in range(NC - 1):
+            e = step(k, e)
         for c in range(2):
             for x in range(ngx):
                 m["padded"][x + 2, c, 8 : 8 + rows2] = e[c][x]

time: 47.8 us -> 47.6 us (level)
  no operation moved by 1% of the time
where the time goes in v8:
time: 47.6 us; the launch traced here: 47.4 us
  Pallas kernels  45.9 us (96%)
  local copies, waits for them, and re-layouts  1.54 us (3%)
    pallas_call x1, Pallas kernels, local(): pl.pallas_call(functools.partial(kernel, ngx, ngy, depth, tree), out_shap...  45.9 us
    unnamed x1, local copies, waits for them, and re-layouts  1.54 us

profile of v8, /device:TPU:0, one launch (start us, length us, event | category | flops | bytes accessed | tf_op | source)
XLA Modules:
  0.0 47.4 jit_solution(3492133546199067093)
XLA Ops:
  0.0 45.9 %shard_map.46 = f32[2,4,8,384]{3,2,1,0:T(8,128)} custom-call(f32[2,4,8,384]{3,2,1,0:T(8,128)} %rhs_in.1, f32[16]{0:T(128)} %table_in.1, s32[4,8,384]{2,1,0:T(8,128)} %layer_in.1, s32[4,8,384]{2,1,0:T(8,128)} %absorb_in.1), custom_call_target="tpu_custom_call" | custom-call | tf_op jit(solution)/shard_map/pallas_call | solution.py:605
  45.9 1.5 %copy.6 = f32[2,4,8,384]{3,2,1,0:T(8,128)} copy(f32[2,4,8,384]{3,2,1,0:T(8,128)} %shard_map.46) | data formatting | bytes 196608
